TPU v7x, 128 devices: a whole 4x4x4 slice. The times are simulated.
128 devices in a mesh: freq: 16 (over x_hi, y, core), stn: 8 (over x_lo, z).
Axes of the slice: x: 4 (x_hi: 2, x_lo: 2; x = x_hi * 2 + x_lo), y: 4, z: 4, core: 2. Of those that a mesh axis runs over, the one named last changes fastest.
Arguments:
- voltages: bfloat16 [1024, 32, 4096], P('stn', 'freq'), may hold values from -6 to 6
- filter_taps: float32 [16, 4096], replicated, may hold values from -1.5 to 1.5
- station_flags: int32 [512, 32], replicated, may hold values from 0 to 1, as said below
Outputs:
- visibilities: float32 [256, 1024, 1024], P('freq', 'stn')
Inputs may be any that keep to these rules, and one draw needn't show every extreme that they name: `station_flags`: 1 keeps a station's data in that spectrum, 0 flags it.
All inputs are finite; a program needn't handle non-finite values.
Results may differ from a plain program's by a relative error of at most 0.0039.
Values may be sent and summed in bfloat16 or wider, within the bound.
No kernel may reach another device: no remote copies, remote signals or barrier semaphores. Data moves between devices by JAX's collectives and lax.ppermute only.
A program may use at most 192 MiB of HBM per device.

v0:
```python
import math

import jax
import jax.numpy as jnp
from jax import lax
from jax.sharding import PartitionSpec as P

AVG = 16


def from_behind(block, axis, distance):
    devices = range(lax.axis_size(axis))
    route = [(i - distance, i) for i in devices if i - distance in devices]
    return lax.ppermute(block, axis, route)


def dct_four(rows):
    highest = lax.Precision.HIGHEST
    count_rows, channels = rows.shape
    inner_len = 128
    outer_len = channels // inner_len
    positions = jnp.arange(channels).astype(jnp.float32)
    theta = math.pi * positions / (2 * channels)
    real_part = (rows * jnp.cos(theta)).reshape(count_rows, outer_len, inner_len)
    imag_part = (-rows * jnp.sin(theta)).reshape(count_rows, outer_len, inner_len)
    outer_idx = jnp.arange(outer_len, dtype=jnp.int32)
    outer_phase = (
        2
        * math.pi
        * (outer_idx[:, None] * outer_idx[None, :] % outer_len).astype(jnp.float32)
        / outer_len
    )
    outer_cos = jnp.cos(outer_phase)
    outer_sin = jnp.sin(outer_phase)
    section_real = jnp.einsum("pab,ak->pkb", real_part, outer_cos, precision=highest) + jnp.einsum(
        "pab,ak->pkb", imag_part, outer_sin, precision=highest
    )
    section_imag = jnp.einsum("pab,ak->pkb", imag_part, outer_cos, precision=highest) - jnp.einsum(
        "pab,ak->pkb", real_part, outer_sin, precision=highest
    )
    inner_idx = jnp.arange(inner_len, dtype=jnp.int32)
    twist_phase = (
        2 * math.pi * (outer_idx[:, None] * inner_idx[None, :]).astype(jnp.float32) / channels
    )
    twist_cos = jnp.cos(twist_phase)
    twist_sin = jnp.sin(twist_phase)
    twist_real = section_real * twist_cos + section_imag * twist_sin
    twist_imag = section_imag * twist_cos - section_real * twist_sin
    inner_phase = (
        2
        * math.pi
        * (inner_idx[:, None] * inner_idx[None, :] % inner_len).astype(jnp.float32)
        / inner_len
    )
    inner_cos = jnp.cos(inner_phase)
    inner_sin = jnp.sin(inner_phase)
    final_real = jnp.einsum("pkb,bq->pqk", twist_real, inner_cos, precision=highest) + jnp.einsum(
        "pkb,bq->pqk", twist_imag, inner_sin, precision=highest
    )
    final_imag = jnp.einsum("pkb,bq->pqk", twist_imag, inner_cos, precision=highest) - jnp.einsum(
        "pkb,bq->pqk", twist_real, inner_sin, precision=highest
    )
    final_real = final_real.reshape(count_rows, channels)
    final_imag = final_imag.reshape(count_rows, channels)
    post_angle = math.pi * (2 * positions + 1) / (4 * channels)
    return math.sqrt(2.0 / channels) * (
        final_real * jnp.cos(post_angle) + final_imag * jnp.sin(post_angle)
    )


def make_tile(mine, theirs):
    return jnp.einsum("gax,gbx->gab", mine, theirs, preferred_element_type=jnp.float32)


def body(voltages, filter_taps, station_flags):
    sig_dev, spec_dev, channels = voltages.shape
    tap_count = filter_taps.shape[0]
    history_len = tap_count - 1
    reach_count = -(-history_len // spec_dev)
    earlier = []
    for distance in range(1, reach_count + 1):
        needed = min(spec_dev, history_len - (distance - 1) * spec_dev)
        earlier.append(from_behind(voltages[:, spec_dev - needed :, :], "freq", distance))
    frames = jnp.concatenate(earlier[::-1] + [voltages], axis=1)
    window = jnp.zeros((sig_dev, spec_dev, channels), jnp.float32)
    for tap_index in range(tap_count):
        offset = history_len - tap_index
        window = window + filter_taps[tap_index][None, None, :] * frames[
            :, offset : offset + spec_dev, :
        ].astype(jnp.float32)
    channelized = dct_four(window.reshape(sig_dev * spec_dev, channels)).astype(jnp.bfloat16)
    groups_all = channels // AVG
    arranged = (
        channelized.reshape(sig_dev, spec_dev, groups_all, AVG)
        .transpose(2, 0, 1, 3)
        .reshape(groups_all, sig_dev, spec_dev * AVG)
    )
    turned = lax.all_to_all(arranged, "freq", split_axis=0, concat_axis=2, tiled=True)
    signal_flags = jnp.repeat(station_flags, 2, axis=0).astype(jnp.float32)
    position = lax.axis_index("stn")
    own_flags = lax.dynamic_slice_in_dim(signal_flags, position * sig_dev, sig_dev, 0)
    keep = jnp.repeat(own_flags, AVG, axis=1).astype(jnp.bfloat16)
    local = turned * keep[None]
    counts = jnp.dot(own_flags, signal_flags.T, precision=lax.Precision.HIGHEST)
    denominator = AVG * jnp.maximum(counts, 1.0)
    totals = make_tile(local, lax.all_gather(local, "stn", axis=1, tiled=True))
    return totals / denominator[None]


def solution(mesh):
    in_specs = (P("stn", "freq", None), P(), P())
    out_specs = P("freq", "stn", None)
    return jax.shard_map(body, mesh=mesh, in_specs=in_specs, out_specs=out_specs, check_vma=False)
```

profile of v0, /device:TPU:1, one launch (start us, length us, event | category | flops | bytes accessed | tf_op | source)
XLA Modules:
  0.0 907.7 jit_solution(544670661215522051)
XLA Ops:
  6.5 4.7 collective-permute-start
  11.3 3.3 collective-permute-start.1
  14.6 4.1 slice.106
  19.8 4.6 collective-permute-start.7
  24.5 5.2 collective-permute-start.2
  32.3 14.6 %collective-permute-done.7 = bf16[128,1,4096]{2,0,1:T(8,128)(2,1)S(1)} collective-permute-done((bf16[128,1,4096]{2,0,1:T(8,128)(2,1)S(1)}, bf16[128,1,4096]{2,0,1:T(8,128)(2,1)S(1)}, u32[]{:S(2)}, u32[]{:S(2)}) %collective-permute-start.7) | collective-permute-done | bytes 1048608 | tf_op jit(solution)/shard_map/ppermute | solution.py:14
  46.9 62.1 %collective-permute-start.4 = (bf16[128,2,4096]{2,1,0:T(2,128)(2,1)S(1)}, bf16[128,2,4096]{2,1,0:T(2,128)(2,1)}, u32[]{:S(2)}, u32[]{:S(2)}) collective-permute-start(bf16[128,2,4096]{2,1,0:T(2,128)(2,1)S(1)} %copy-done.2), channel_id=1, source_target_pairs={{0,40},{8,48},{16,56},{24,64},{32,72},{40,80},{48,88},{56,96},{64,... | collective-permute-start | bytes 6291464 | tf_op jit(solution)/shard_map/ppermute | solution.py:14
  109.0 65.9 %collective-permute-start.5 = (bf16[128,2,4096]{2,1,0:T(2,128)(2,1)S(1)}, bf16[128,2,4096]{2,1,0:T(2,128)(2,1)}, u32[]{:S(2)}, u32[]{:S(2)}) collective-permute-start(bf16[128,2,4096]{2,1,0:T(2,128)(2,1)S(1)} %copy-done.2), channel_id=1, source_target_pairs={{0,48},{8,56},{16,64},{24,72},{32,80},{40,88},{48,96},{56,104},{64... | collective-permute-start | bytes 6291464 | tf_op jit(solution)/shard_map/ppermute | solution.py:14
  176.3 2.8 collective-permute-start.6
  184.7 4.5 collective-permute-done.3
  189.2 51.1 %collective-permute-done.5 = bf16[128,2,4096]{2,1,0:T(2,128)(2,1)} collective-permute-done((bf16[128,2,4096]{2,1,0:T(2,128)(2,1)S(1)}, bf16[128,2,4096]{2,1,0:T(2,128)(2,1)}, u32[]{:S(2)}, u32[]{:S(2)}) %collective-permute-start.5) | collective-permute-done | bytes 2097184 | tf_op jit(solution)/shard_map/ppermute | solution.py:14
  240.3 61.7 %multiply_add_fusion = f32[128,2,4096]{2,1,0:T(2,128)} fusion(bf16[128,2,4096]{2,1,0:T(2,128)(2,1)} %collective-permute-done.6, bf16[128,2,4096]{2,1,0:T(2,128)(2,1)} %collective-permute-done.5, bf16[128,2,4096]{2,1,0:T(2,128)(2,1)} %collective-permute-done.4, bf16[128,2,4096]{2,1,0:T(2,128)(2,1)} %collective-permute-done.3, ...), kind=kLoop, calls=%fused_computation.8 | loop fusion | flops 74448896 | bytes 22282240 | tf_op jit(solution)/shard_map/add | solution.py:88
  302.0 6.6 reshape.108
  308.6 6.0 fusion.14
  314.6 4.1 fusion.9
  318.7 4.4 fusion.20
  323.1 5.1 add_bitcast_fusion.1
  328.3 6.0 fusion.3
  334.3 8.3 fusion.1
  342.5 8.0 add_bitcast_fusion
  350.5 14.5 %copy.49 = f32[256,128,32]{2,1,0:T(8,128)} copy(f32[256,128,32]{0,1,2:T(8,128)} %add_bitcast_fusion) | data formatting | bytes 8388608 | tf_op jit(solution)/shard_map/add | solution.py:57
  365.0 24.6 %reshape.109 = f32[128,2,256,16]{3,2,1,0:T(8,128)} reshape(f32[256,128,32]{2,1,0:T(8,128)} %copy.49) | data formatting | bytes 8388608 | tf_op jit(solution)/shard_map/reshape | solution.py:63
  389.7 11.4 %subtract_bitcast_fusion = f32[256,128,32]{0,1,2:T(8,128)} fusion(f32[128,256,32]{1,0,2:T(8,128)} %fusion.1, f32[256,32,128]{2,1,0:T(8,128)} %copy-done.1), kind=kOutput, calls=%fused_computation.3 | convolution fusion | flops 1611890688 | bytes 12582912 | tf_op jit(solution)/shard_map/pkb,bq->pqk/dot_general | solution.py:60
  401.1 14.5 %copy.53 = f32[256,128,32]{2,1,0:T(8,128)} copy(f32[256,128,32]{0,1,2:T(8,128)} %subtract_bitcast_fusion) | data formatting | bytes 8388608 | tf_op jit(solution)/shard_map/sub | solution.py:60
  415.7 24.4 %reshape.110 = f32[128,2,256,16]{3,2,1,0:T(8,128)} reshape(f32[256,128,32]{2,1,0:T(8,128)} %copy.53) | data formatting | bytes 8388608 | tf_op jit(solution)/shard_map/reshape | solution.py:64
  440.1 27.8 %fusion = bf16[256,128,2,16]{3,0,2,1:T(8,128)(2,1)} fusion(f32[128,2,256,16]{3,2,1,0:T(8,128)} %reshape.110, f32[128,2,256,16]{3,2,1,0:T(8,128)} %reshape.109, f32[256,16]{1,0:T(8,128)S(1)} %copy.54, f32[256,16]{1,0:T(8,128)S(1)} %copy.50), kind=kLoop, calls=%fused_computation.1 | loop fusion | flops 5242880 | bytes 10518528 | tf_op jit(solution)/shard_map/transpose | solution.py:95
  467.8 15.4 %copy.55 = bf16[256,128,2,16]{1,3,2,0:T(8,128)(2,1)} copy(bf16[256,128,2,16]{3,0,2,1:T(8,128)(2,1)} %fusion) | data formatting | bytes 4194304 | tf_op jit(solution)/shard_map/transpose | solution.py:95
  483.2 197.7 %all-to-all-start = ((bf16[256,128,32]{1,2,0:T(8,128)(2,1)}), bf16[256,128,32]{1,2,0:T(8,128)(2,1)S(1)}, u32[]{:S(2)}, u32[]{:S(2)}) async-start(bf16[256,128,32]{1,2,0:T(8,128)(2,1)} %bitcast.25), calls=%async_computation | async-start | bytes 4194304 | tf_op jit(solution)/shard_map/all_to_all | solution.py:98
  681.6 27.8 %all-to-all-done = bf16[256,128,32]{1,2,0:T(8,128)(2,1)S(1)} async-done(((bf16[256,128,32]{1,2,0:T(8,128)(2,1)}), bf16[256,128,32]{1,2,0:T(8,128)(2,1)S(1)}, u32[]{:S(2)}, u32[]{:S(2)}) %all-to-all-start) | async-done | bytes 2097184 | tf_op jit(solution)/shard_map/all_to_all | solution.py:98
  711.3 3.1 copy.60
  716.5 172.2 %all-gather.2.cloned.1.call-done = bf16[16,1024,512]{2,1,0:T(8,128)(2,1)} async-done(((bf16[16,128,512]{2,1,0:T(8,128)(2,1)}), bf16[16,1024,512]{2,1,0:T(8,128)(2,1)}) %all-gather.2.cloned.1.call-update) | async-done | bytes 16777232 | tf_op jit(solution)/shard_map/all_gather | solution.py:106
  888.7 11.7 %broadcast_divide_fusion = f32[16,128,1024]{2,1,0:T(8,128)} fusion(f32[128,1024]{1,0:T(8,128)S(1)} %fusion.27, bf16[16,128,512]{2,1,0:T(8,128)(2,1)} %broadcast_multiply_fusion, bf16[16,1024,512]{2,1,0:T(8,128)(2,1)} %all-gather.2.cloned.1.call-done), kind=kOutput, calls=%fused_computation.2 | convolution fusion | flops 2149580800 | bytes 27787264 | tf_op jit(solution)/shard_map/gax,gbx->gab/dot_general | solution.py:72
  (42 shorter events, 15.2 us)
Async XLA Ops:
  6.5 17.9 %copy-start.2 = (bf16[128,2,4096]{2,1,0:T(2,128)(2,1)S(1)}, bf16[128,2,4096]{2,1,0:T(2,128)(2,1)}, u32[]{:S(2)}) copy-start(bf16[128,2,4096]{2,1,0:T(2,128)(2,1)} %param.3) | copy-start | bytes 6291460
  6.5 102.5 %collective-permute-start = (bf16[128,2,4096]{2,1,0:T(2,128)(2,1)}, bf16[128,2,4096]{2,1,0:T(2,128)(2,1)S(1)}, u32[]{:S(2)}, u32[]{:S(2)}) collective-permute-start(bf16[128,2,4096]{2,1,0:T(2,128)(2,1)} %param.3), channel_id=1, source_target_pairs={{0,8},{8,16},{16,24},{24,32},{32,40},{40,48},{48,56},{56,64},{64,7... | collective-permute-start | bytes 6291464 | tf_op jit(solution)/shard_map/ppermute | solution.py:14
  11.3 163.7 %collective-permute-start.1 = (bf16[128,2,4096]{2,1,0:T(2,128)(2,1)}, bf16[128,2,4096]{2,1,0:T(2,128)(2,1)S(1)}, u32[]{:S(2)}, u32[]{:S(2)}) collective-permute-start(bf16[128,2,4096]{2,1,0:T(2,128)(2,1)} %param.3), channel_id=1, source_target_pairs={{0,16},{8,24},{16,32},{24,40},{32,48},{40,56},{48,64},{56,72},{64,... | collective-permute-start | bytes 6291464 | tf_op jit(solution)/shard_map/ppermute | solution.py:14
  19.8 27.1 %collective-permute-start.7 = (bf16[128,1,4096]{2,0,1:T(8,128)(2,1)S(1)}, bf16[128,1,4096]{2,0,1:T(8,128)(2,1)S(1)}, u32[]{:S(2)}, u32[]{:S(2)}) collective-permute-start(bf16[128,1,4096]{2,0,1:T(8,128)(2,1)S(1)} %copy.61), channel_id=1, source_target_pairs={{0,64},{8,72},{16,80},{24,88},{32,96},{40,104},{48,112},{56,120},{... | collective-permute-start | bytes 3145736 | tf_op jit(solution)/shard_map/ppermute | solution.py:14
  24.5 160.2 %collective-permute-start.2 = (bf16[128,2,4096]{2,1,0:T(2,128)(2,1)S(1)}, bf16[128,2,4096]{2,1,0:T(2,128)(2,1)}, u32[]{:S(2)}, u32[]{:S(2)}) collective-permute-start(bf16[128,2,4096]{2,1,0:T(2,128)(2,1)S(1)} %copy-done.2), channel_id=1, source_target_pairs={{0,24},{8,32},{16,40},{24,48},{32,56},{40,64},{48,72},{56,80},{64,... | collective-permute-start | bytes 6291464 | tf_op jit(solution)/shard_map/ppermute | solution.py:14
  29.7 159.5 %collective-permute-start.3 = (bf16[128,2,4096]{2,1,0:T(2,128)(2,1)S(1)}, bf16[128,2,4096]{2,1,0:T(2,128)(2,1)}, u32[]{:S(2)}, u32[]{:S(2)}) collective-permute-start(bf16[128,2,4096]{2,1,0:T(2,128)(2,1)S(1)} %copy-done.2), channel_id=1, source_target_pairs={{0,32},{8,40},{16,48},{24,56},{32,64},{40,72},{48,80},{56,88},{64,... | collective-permute-start | bytes 6291464 | tf_op jit(solution)/shard_map/ppermute | solution.py:14
  46.9 142.3 %collective-permute-start.4 = (bf16[128,2,4096]{2,1,0:T(2,128)(2,1)S(1)}, bf16[128,2,4096]{2,1,0:T(2,128)(2,1)}, u32[]{:S(2)}, u32[]{:S(2)}) collective-permute-start(bf16[128,2,4096]{2,1,0:T(2,128)(2,1)S(1)} %copy-done.2), channel_id=1, source_target_pairs={{0,40},{8,48},{16,56},{24,64},{32,72},{40,80},{48,88},{56,96},{64,... | collective-permute-start | bytes 6291464 | tf_op jit(solution)/shard_map/ppermute | solution.py:14
  109.0 65.9 %copy-start.3 = (bf16[128,2,4096]{2,1,0:T(2,128)(2,1)}, bf16[128,2,4096]{2,1,0:T(2,128)(2,1)S(1)}, u32[]{:S(2)}) copy-start(bf16[128,2,4096]{2,1,0:T(2,128)(2,1)S(1)} %collective-permute-done) | copy-start | bytes 6291460
  109.0 131.3 %collective-permute-start.5 = (bf16[128,2,4096]{2,1,0:T(2,128)(2,1)S(1)}, bf16[128,2,4096]{2,1,0:T(2,128)(2,1)}, u32[]{:S(2)}, u32[]{:S(2)}) collective-permute-start(bf16[128,2,4096]{2,1,0:T(2,128)(2,1)S(1)} %copy-done.2), channel_id=1, source_target_pairs={{0,48},{8,56},{16,64},{24,72},{32,80},{40,88},{48,96},{56,104},{64... | collective-permute-start | bytes 6291464 | tf_op jit(solution)/shard_map/ppermute | solution.py:14
  174.9 1.3 copy-start.5
  176.3 64.1 %collective-permute-start.6 = (bf16[128,2,4096]{2,1,0:T(2,128)(2,1)S(1)}, bf16[128,2,4096]{2,1,0:T(2,128)(2,1)}, u32[]{:S(2)}, u32[]{:S(2)}) collective-permute-start(bf16[128,2,4096]{2,1,0:T(2,128)(2,1)S(1)} %copy-done.2), channel_id=1, source_target_pairs={{0,56},{8,64},{16,72},{24,80},{32,88},{40,96},{48,104},{56,112},{6... | collective-permute-start | bytes 6291464 | tf_op jit(solution)/shard_map/ppermute | solution.py:14
  179.4 60.9 %copy-start.4 = (bf16[128,2,4096]{2,1,0:T(2,128)(2,1)S(1)}, bf16[128,2,4096]{2,1,0:T(2,128)(2,1)}, u32[]{:S(2)}) copy-start(bf16[128,2,4096]{2,1,0:T(2,128)(2,1)} %copy-done.3) | copy-start | bytes 6291460
  308.6 6.0 copy-start
  328.2 14.3 %copy-start.1 = (f32[256,32,128]{2,1,0:T(8,128)}, f32[256,32,128]{2,1,0:T(8,128)S(1)}, u32[]{:S(2)}) copy-start(f32[256,32,128]{2,1,0:T(8,128)S(1)} %get-tuple-element.5) | copy-start | bytes 12582916
  483.2 197.7 %copy-start.6 = (s32[512,32]{0,1:T(8,128)S(1)}, s32[512,32]{0,1:T(8,128)}, u32[]{:S(2)}) copy-start(s32[512,32]{0,1:T(8,128)} %param.5) | copy-start | bytes 196612
  483.2 226.2 %all-to-all-start = ((bf16[256,128,32]{1,2,0:T(8,128)(2,1)}), bf16[256,128,32]{1,2,0:T(8,128)(2,1)S(1)}, u32[]{:S(2)}, u32[]{:S(2)}) async-start(bf16[256,128,32]{1,2,0:T(8,128)(2,1)} %bitcast.25), calls=%async_computation | async-start | bytes 4194304 | tf_op jit(solution)/shard_map/all_to_all | solution.py:98
  680.9 207.8 %all-gather.2.cloned.1.call-start = ((), (), s32[]{:S(2)}) async-start(), calls=%async_computation.1 | async-start | bytes 18874368 | tf_op jit(solution)/shard_map/all_gather | solution.py:106
Sparse Core Ops, SparseCore 0:
  716.0 172.6 all-gather.1
where the time goes:
time: 914 us; the launch traced here: 908 us
  starting transfers between devices  349 us (38%)
  waiting for transfers between devices  270 us (30%)
  local copies, waits for them, and re-layouts  117 us (13%)
  other arithmetic  91.3 us (10%)
  matrix products  65.6 us (7%)
  between operations  14.2 us (2%)
    all_to_all x1, starting transfers between devices, body(): lax.all_to_all(arranged, 'freq', split_axis=0, concat_axis=2, tiled=True)  198 us
    all_gather x1, waiting for transfers between devices, body(): totals = make_tile(local, lax.all_gather(local, 'stn', axis=1, tiled=True))  172 us
    ppermute x8, starting transfers between devices, from_behind(): return lax.ppermute(block, axis, route)  151 us
    ppermute x8, waiting for transfers between devices, from_behind(): return lax.ppermute(block, axis, route)  70.3 us
    add x1, other arithmetic, body(): window + filter_taps[tap_index][None, None, :] * frames[:, offset:offset...  61.7 us
    all_to_all x1, waiting for transfers between devices, body(): lax.all_to_all(arranged, 'freq', split_axis=0, concat_axis=2, tiled=True)  27.8 us
    transpose x1, other arithmetic, body(): arranged = channelized.reshape(sig_dev, spec_dev, groups_all, AVG).transp...  27.8 us
    reshape x1, local copies, waits for them, and re-layouts, dct_four(): final_real = final_real.reshape(count_rows, channels)  24.6 us
  transfers between devices with their start and end apart: 10, of which 5 were waited for; matrix products, arithmetic and copies ran while one was open for 1% of the time, Pallas kernels for 0%

commit v1 on v0

v1 whole, which is shorter than its diff:
```python
import math

import jax
import jax.numpy as jnp
import numpy as np
from jax import lax
from jax.experimental import pallas as pl
from jax.experimental.pallas import tpu as pltpu
from jax.sharding import PartitionSpec as P

AVG = 16
LANES = 128
INNER = 256
F32 = jnp.float32
BF16 = jnp.bfloat16


def transform_tables(channels, n_freq, n_stn):
    j0 = np.arange(INNER, dtype=np.float64)
    k1 = np.arange(AVG, dtype=np.float64)
    phase = 2 * np.pi * k1[:, None] * j0[None, :] / channels + np.pi * j0[None, :] / (2 * channels)
    phase = phase + np.pi * (2 * k1[:, None] + 1) / (4 * channels)
    twiddle = np.stack([np.cos(phase), -np.sin(phase)]).astype(np.float32)
    groups = channels // AVG
    per_device = groups // (n_freq * n_stn)
    k2 = np.arange(groups).reshape(n_freq, n_stn, per_device).transpose(1, 0, 2).reshape(-1)
    phase = 2 * np.pi * (k2[:, None] * np.arange(INNER)[None, :] % INNER) / INNER
    phase = phase + 2 * np.pi * AVG * k2[:, None] / (4 * channels)
    scale = math.sqrt(2.0 / channels)
    exact = np.concatenate([np.cos(phase), np.sin(phase)], axis=1) * scale
    exact = jnp.asarray(exact.astype(np.float32))
    high = exact.astype(BF16)
    low = (exact - high.astype(F32)).astype(BF16)
    return jnp.asarray(twiddle), jnp.concatenate([high, high, low], axis=1)


def times(value, angle):
    c, s = math.cos(angle), math.sin(angle)
    re, im = value
    return re * c + im * s, im * c - re * s


def four_point(u0, u1, u2, u3):
    def add(a, b):
        return a[0] + b[0], a[1] + b[1]

    def sub(a, b):
        return a[0] - b[0], a[1] - b[1]

    s0, s1, t0, t1 = add(u0, u2), sub(u0, u2), add(u1, u3), sub(u1, u3)
    return add(s0, t0), (s1[0] + t1[1], s1[1] - t1[0]), sub(s0, t0), (s1[0] - t1[1], s1[1] + t1[0])


def sixteen_point(x):
    mid = []
    for b in range(4):
        u = [(x[b], jnp.zeros_like(x[b]))]
        for a in range(1, 4):
            angle = math.pi * a / 8
            u.append((x[4 * a + b] * math.cos(angle), x[4 * a + b] * -math.sin(angle)))
        row = four_point(*u)
        mid.append([times(row[p], 2 * math.pi * b * p / 16 + math.pi * b / 32) if b else row[p] for p in range(4)])
    y = [None] * 16
    for p in range(4):
        out = four_point(*[mid[b][p] for b in range(4)])
        for q in range(4):
            y[p + 4 * q] = out[q]
    return y


def channelize_kernel(x_ref, taps_ref, twiddle_ref, second_ref, keep_ref, out_ref, window, stage, turned):
    frames, signals, channels = x_ref.shape
    taps = taps_ref.shape[0]
    groups = second_ref.shape[0]

    def fir(block, carry):
        lanes = pl.ds(pl.multiple_of(block * LANES, LANES), LANES)
        tap = [jnp.broadcast_to(taps_ref[pl.ds(t, 1), lanes], (signals, LANES)) for t in range(taps)]
        x = [x_ref[m, :, lanes].astype(F32) for m in range(frames)]
        for m in range(frames):
            total = tap[0] * x[m]
            for t in range(1, min(taps, m + 1)):
                total = total + tap[t] * x[m - t]
            window[m, :, lanes] = total
        return carry

    lax.fori_loop(0, channels // LANES, fir, 0)

    def first(m, carry):
        for half in range(INNER // LANES):
            at = pl.ds(half * LANES, LANES)
            x = [window[m, :, pl.ds(j1 * INNER + half * LANES, LANES)] for j1 in range(AVG)]
            for k1, y in enumerate(sixteen_point(x)):
                tre = twiddle_ref[0, pl.ds(k1, 1), at]
                tim = twiddle_ref[1, pl.ds(k1, 1), at]
                rows = pl.ds(pl.multiple_of(k1 * frames * signals + m * signals, signals), signals)
                stage[half, rows, :] = y[0] * tre - y[1] * tim
                stage[INNER // LANES + half, rows, :] = y[0] * tim + y[1] * tre
        return carry

    lax.fori_loop(0, frames, first, 0)

    columns = AVG * frames
    for i in range(signals):
        y = jnp.concatenate([stage[part, pl.ds(i, columns, stride=signals), :] for part in range(4)], axis=1)
        high = y.astype(BF16)
        low = (y - high.astype(F32)).astype(BF16)
        z = lax.dot_general(
            second_ref[...],
            jnp.concatenate([high, low, high], axis=1),
            (((1,), (1,)), ((), ())),
            preferred_element_type=F32,
        )
        for c in range(columns // LANES):
            turned[c, pl.ds(i, groups, stride=signals), :] = z[:, c * LANES : (c + 1) * LANES]

    keep = keep_ref[...]

    def last(step, carry):
        rows = pl.ds(pl.multiple_of(step * 32 * signals, 32 * signals), 32 * signals)
        for c in range(columns // LANES):
            value = turned[c, rows, :].reshape(16, 2, signals, LANES) * keep[None, None]
            for pair in range(2):
                part = value[:, pair].reshape(16 * signals, LANES).astype(BF16)
                to = pl.ds(pl.multiple_of(step * 16 * signals, 16 * signals), 16 * signals)
                out_ref[to, pair * columns + c * LANES : pair * columns + (c + 1) * LANES] = part
        return carry

    lax.fori_loop(0, groups // 32, last, 0)


def channelize(x, taps, twiddle, second, keep):
    frames, signals, channels = x.shape
    groups = channels // AVG
    columns = AVG * frames
    whole = pl.BlockSpec(memory_space=pltpu.VMEM)
    return pl.pallas_call(
        channelize_kernel,
        out_shape=jax.ShapeDtypeStruct((groups // 2 * signals, 2 * columns), BF16),
        in_specs=[whole] * 5,
        out_specs=whole,
        scratch_shapes=[
            pltpu.VMEM((frames, signals, channels), F32),
            pltpu.VMEM((4, AVG * frames * signals, LANES), F32),
            pltpu.VMEM((columns // LANES, groups * signals, LANES), F32),
        ],
        compiler_params=pltpu.CompilerParams(vmem_limit_bytes=50 * 1024 * 1024),
        name="channelize",
    )(x, taps, twiddle, second, keep)


def correlate_kernel(rows_ref, all_ref, out_ref):
    columns = rows_ref.shape[1] // 2
    for pair in range(2):
        at = slice(pair * columns, (pair + 1) * columns)
        out_ref[0, pair] = lax.dot_general(
            rows_ref[:, at], all_ref[:, at], (((1,), (1,)), ((), ())), preferred_element_type=F32
        ).astype(BF16)


def correlate(data, n_stn):
    signals, width = data.shape
    rows = signals // n_stn
    return pl.pallas_call(
        correlate_kernel,
        out_shape=jax.ShapeDtypeStruct((n_stn, 2, rows, signals), BF16),
        grid=(n_stn,),
        in_specs=[
            pl.BlockSpec((rows, width), lambda d: (d, 0)),
            pl.BlockSpec((signals, width), lambda d: (0, 0)),
        ],
        out_specs=pl.BlockSpec((1, 2, rows, signals), lambda d: (d, 0, 0, 0)),
        compiler_params=pltpu.CompilerParams(vmem_limit_bytes=50 * 1024 * 1024),
        name="correlate",
    )(data, data)


def body(voltages, filter_taps, station_flags):
    sig_dev, spec_dev, channels = voltages.shape
    n_freq, n_stn = lax.axis_size("freq"), lax.axis_size("stn")
    own = sig_dev // n_freq
    frames = n_freq * spec_dev
    flags = jnp.repeat(station_flags, 2, axis=0).astype(F32)
    at_freq, at_stn = lax.axis_index("freq"), lax.axis_index("stn")
    keep = lax.dynamic_slice_in_dim(flags, at_stn * sig_dev + at_freq * own, own, 0)
    keep = jnp.tile(keep, (1, LANES // frames))
    twiddle, second = transform_tables(channels, n_freq, n_stn)

    x = lax.all_to_all(voltages.reshape(n_freq, own, spec_dev, channels), "freq", split_axis=0, concat_axis=0, tiled=True)
    x = x.transpose(0, 2, 1, 3).reshape(frames, own, channels)
    kept = channelize(x, filter_taps, twiddle, second, keep)
    data = lax.all_to_all(kept, ("stn", "freq"), split_axis=0, concat_axis=0, tiled=True)
    sums = correlate(data, n_stn)
    sums = lax.all_to_all(sums, "stn", split_axis=0, concat_axis=0, tiled=True)
    own_flags = lax.dynamic_slice_in_dim(flags, at_stn * sig_dev, sig_dev, 0)
    counts = jnp.dot(own_flags, flags.T, precision=lax.Precision.HIGHEST)
    scale = 1.0 / (AVG * jnp.maximum(counts, 1.0))
    return sums.reshape(n_stn * 2, sig_dev, -1).astype(F32) * scale[None]


def solution(mesh):
    in_specs = (P("stn", "freq", None), P(), P())
    out_specs = P("freq", "stn", None)
    return jax.shard_map(body, mesh=mesh, in_specs=in_specs, out_specs=out_specs, check_vma=False)
```

time: 914 us -> 165 us (0.18)
  starting transfers between devices: 349 us -> 13.1 us
  waiting for transfers between devices: 270 us -> 75.2 us
  local copies, waits for them, and re-layouts: 117 us -> 6.81 us
  other arithmetic: 91.3 us -> 6.8 us
  matrix products: 65.6 us -> 0.61 us
  blocking collectives: 0 us -> 40.5 us
  Pallas kernels: 0 us -> 21.3 us
  between operations: 14.2 us -> 0.1 us
    all_to_all x1 -> x2, starting transfers between devices: 198 us -> 13.1 us  [the longest x1 8.45 us: body(): lax.all_to_all(voltages.reshape(n_freq, own, spec_dev, channels), 'freq',...]
    all_gather x1 -> x0, waiting for transfers between devices: 172 us -> none  [body(): totals = make_tile(local, lax.all_gather(local, 'stn', axis=1, tiled=True))]
    ppermute x8 -> x0, starting transfers between devices: 151 us -> none  [from_behind(): return lax.ppermute(block, axis, route)]
    ppermute x8 -> x0, waiting for transfers between devices: 70.3 us -> none  [from_behind(): return lax.ppermute(block, axis, route)]
    dot_general x10 -> x1, matrix products: 65.6 us -> 0.61 us  [body(): counts = jnp.dot(own_flags, flags.T, precision=lax.Precision.HIGHEST)]
    add x1 -> x0, other arithmetic: 61.7 us -> none  [body(): window + filter_taps[tap_index][None, None, :] * frames[:, offset:offset...]
    reshape x3 -> x1, local copies, waits for them, and re-layouts: 55.7 us -> 4.29 us  [body(): voltages.reshape(n_freq, own, spec_dev, channels)]
    all_to_all x1 -> x2, waiting for transfers between devices: 27.8 us -> 75.2 us  [the longest x1 48 us: body(): sums = lax.all_to_all(sums, 'stn', split_axis=0, concat_axis=0, tiled=True)]
  transfers between devices with their start and end apart: 10 -> 2, of which waited for: 5 -> 2; matrix products, arithmetic and copies ran while one was open for 1% -> 1% of each run, Pallas kernels for 0% -> 0%
where the time goes in v1:
time: 165 us
  waiting for transfers between devices  75.2 us (46%)
  blocking collectives  40.5 us (25%)
  Pallas kernels  21.3 us (13%)
  starting transfers between devices  13.1 us (8%)
  local copies, waits for them, and re-layouts  6.81 us (4%)
  other arithmetic  6.8 us (4%)
    all_to_all x1, waiting for transfers between devices, body(): sums = lax.all_to_all(sums, 'stn', split_axis=0, concat_axis=0, tiled=True)  48 us
    all_to_all x1, blocking collectives, body(): lax.all_to_all(kept, ('stn', 'freq'), split_axis=0, concat_axis=0, tiled=...  40.5 us
    all_to_all x1, waiting for transfers between devices, body(): lax.all_to_all(voltages.reshape(n_freq, own, spec_dev, channels), 'freq',...  27.2 us
    pallas_call x1, Pallas kernels, channelize(): pl.pallas_call(channelize_kernel, out_shape=jax.ShapeDtypeStruct((groups...  13.9 us
    all_to_all x1, starting transfers between devices, body(): lax.all_to_all(voltages.reshape(n_freq, own, spec_dev, channels), 'freq',...  8.45 us
    pallas_call x1, Pallas kernels, correlate(): pl.pallas_call(correlate_kernel, out_shape=jax.ShapeDtypeStruct((n_stn, 2...  7.45 us
    mul x1, other arithmetic, body(): return sums.reshape(n_stn * 2, sig_dev, -1).astype(F32) * scale[None]  6.8 us
    all_to_all x1, starting transfers between devices, body(): sums = lax.all_to_all(sums, 'stn', split_axis=0, concat_axis=0, tiled=True)  4.68 us
  transfers between devices with their start and end apart: 2, of which 2 were waited for; matrix products, arithmetic and copies ran while one was open for 1% of the time, Pallas kernels for 0%

profile of v1, /device:TPU:1, one launch (start us, length us, event | category | flops | bytes accessed | tf_op | source)
XLA Modules:
  0.0 164.5 jit_solution(7400137003091179246)
XLA Ops:
  0.0 0.0 copy-start.6
  0.0 0.0 copy-start
  0.0 0.0 copy-start.1
  0.0 0.0 copy-start.2
  0.0 4.3 %copy.6 = bf16[16,8,2,4096]{3,1,2,0:T(8,128)(2,1)} copy(bf16[16,8,2,4096]{3,2,1,0:T(2,128)(2,1)} %bitcast.15) | data formatting | bytes 4194304 | tf_op jit(solution)/shard_map/reshape | solution.py:189
  4.3 8.4 %all-to-all-start = ((bf16[16,8,2,4096]{3,1,2,0:T(8,128)(2,1)}), bf16[16,8,2,4096]{3,1,2,0:T(8,128)(2,1)S(1)}, u32[]{:S(2)}, u32[]{:S(2)}) async-start(bf16[16,8,2,4096]{3,1,2,0:T(8,128)(2,1)} %copy.6), calls=%async_computation | async-start | bytes 4194304 | tf_op jit(solution)/shard_map/all_to_all | solution.py:189
  12.8 0.0 copy-done.6
  12.8 0.1 copy.7
  12.9 0.2 broadcast_in_dim.4
  13.1 0.0 copy-start.4
  13.1 0.8 copy-done.4
  13.9 0.1 tile.10.keep_ref
  14.0 27.2 %all-to-all-done = bf16[16,8,2,4096]{3,1,2,0:T(8,128)(2,1)S(1)} async-done(((bf16[16,8,2,4096]{3,1,2,0:T(8,128)(2,1)}), bf16[16,8,2,4096]{3,1,2,0:T(8,128)(2,1)S(1)}, u32[]{:S(2)}, u32[]{:S(2)}) %all-to-all-start) | async-done | bytes 2097184 | tf_op jit(solution)/shard_map/all_to_all | solution.py:189
  41.2 0.0 copy-start.3
  41.2 1.3 copy-done.3
  42.6 0.0 copy-done
  42.6 0.0 copy-done.1
  42.6 0.0 copy-done.2
  42.6 13.9 %channelize.1 = bf16[1024,1024]{1,0:T(8,128)(2,1)S(1)} custom-call(bf16[32,8,4096]{2,1,0:T(8,128)(2,1)} %bitcast.14, f32[16,4096]{1,0:T(8,128)S(1)} %copy-done.1, f32[2,16,256]{2,1,0:T(8,128)S(1)} %copy-done.2, bf16[256,1536]{1,0:T(8,128)(2,1)S(1)} %copy-done, f32[8,128]{1,0:T(8,128)S(1)} %tile.10.keep_ref), custom_call_target="tpu_custom_call" | custom-call | tf_op jit(solution)/shard_map/channelize/pallas_call | solution.py:137
  56.4 40.5 %all_to_all.21 = bf16[128,8,1024]{2,1,0:T(8,128)(2,1)S(1)} all-to-all(bf16[128,8,1024]{2,1,0:T(8,128)(2,1)S(1)} %bitcast.13), channel_id=1, replica_groups=mesh['freq'=16,'stn'=8] {'stn','freq'}, dimensions={0} | all-to-all | bytes 4194304 | tf_op jit(solution)/shard_map/all_to_all | solution.py:192
  96.9 7.4 %correlate.1 = bf16[8,2,128,1024]{3,2,1,0:T(8,128)(2,1)} custom-call(bf16[1024,1024]{1,0:T(8,128)(2,1)S(1)} %bitcast.11, bf16[1024,1024]{1,0:T(8,128)(2,1)S(1)} %bitcast.12), custom_call_target="tpu_custom_call" | custom-call | tf_op jit(solution)/shard_map/correlate/pallas_call | solution.py:164
  104.4 0.0 copy-start.5
  104.4 4.7 %all-to-all-start.2 = ((bf16[8,2,128,1024]{3,2,1,0:T(8,128)(2,1)}), bf16[8,2,128,1024]{3,2,1,0:T(8,128)(2,1)}, u32[]{:S(2)}, u32[]{:S(2)}) async-start(bf16[8,2,128,1024]{3,2,1,0:T(8,128)(2,1)} %correlate.1), calls=%async_computation.2 | async-start | bytes 8388608 | tf_op jit(solution)/shard_map/all_to_all | solution.py:194
  109.1 0.0 copy-done.5
  109.1 0.6 fusion.1
  109.7 48.0 %all-to-all-done.2 = bf16[8,2,128,1024]{3,2,1,0:T(8,128)(2,1)} async-done(((bf16[8,2,128,1024]{3,2,1,0:T(8,128)(2,1)}), bf16[8,2,128,1024]{3,2,1,0:T(8,128)(2,1)}, u32[]{:S(2)}, u32[]{:S(2)}) %all-to-all-start.2) | async-done | bytes 4194336 | tf_op jit(solution)/shard_map/all_to_all | solution.py:194
  157.7 6.8 %convert_multiply_fusion = f32[16,128,1024]{2,1,0:T(8,128)} fusion(bf16[8,2,128,1024]{3,2,1,0:T(8,128)(2,1)} %all-to-all-done.2, f32[128,1024]{1,0:T(8,128)S(1)} %fusion.1), kind=kLoop, calls=%fused_computation | loop fusion | flops 4194304 | bytes 13107200 | tf_op jit(solution)/shard_map/mul | solution.py:198
  (3 shorter events, 0.0 us)
Async XLA Ops:
  0.0 12.8 %copy-start.6 = (s32[512,32]{0,1:T(8,128)S(1)}, s32[512,32]{0,1:T(8,128)}, u32[]{:S(2)}) copy-start(s32[512,32]{0,1:T(8,128)} %param.7) | copy-start | bytes 196612
  0.0 42.6 %copy-start = (bf16[256,1536]{1,0:T(8,128)(2,1)S(1)}, bf16[256,1536]{1,0:T(8,128)(2,1)}, u32[]{:S(2)}) copy-start(bf16[256,1536]{1,0:T(8,128)(2,1)} %constant.32.second_ref) | copy-start | bytes 2359300
  0.0 42.6 %copy-start.1 = (f32[16,4096]{1,0:T(8,128)S(1)}, f32[16,4096]{1,0:T(8,128)}, u32[]{:S(2)}) copy-start(f32[16,4096]{1,0:T(8,128)} %taps_ref.1) | copy-start | bytes 786436
  0.0 42.6 %copy-start.2 = (f32[2,16,256]{2,1,0:T(8,128)S(1)}, f32[2,16,256]{2,1,0:T(8,128)}, u32[]{:S(2)}) copy-start(f32[2,16,256]{2,1,0:T(8,128)} %constant.26.clone.twiddle_ref) | copy-start | bytes 98308
  4.3 36.9 %all-to-all-start = ((bf16[16,8,2,4096]{3,1,2,0:T(8,128)(2,1)}), bf16[16,8,2,4096]{3,1,2,0:T(8,128)(2,1)S(1)}, u32[]{:S(2)}, u32[]{:S(2)}) async-start(bf16[16,8,2,4096]{3,1,2,0:T(8,128)(2,1)} %copy.6), calls=%async_computation | async-start | bytes 4194304 | tf_op jit(solution)/shard_map/all_to_all | solution.py:189
  13.1 0.8 copy-start.4
  41.2 1.3 copy-start.3
  104.4 4.7 %copy-start.5 = (f32[512,2,32]{2,1,0:T(2,128)S(1)}, f32[512,2,32]{2,1,0:T(2,128)}, u32[]{:S(2)}) copy-start(f32[512,2,32]{2,1,0:T(2,128)} %copy-done.4) | copy-start | bytes 393220
  104.4 53.3 %all-to-all-start.2 = ((bf16[8,2,128,1024]{3,2,1,0:T(8,128)(2,1)}), bf16[8,2,128,1024]{3,2,1,0:T(8,128)(2,1)}, u32[]{:S(2)}, u32[]{:S(2)}) async-start(bf16[8,2,128,1024]{3,2,1,0:T(8,128)(2,1)} %correlate.1), calls=%async_computation.2 | async-start | bytes 8388608 | tf_op jit(solution)/shard_map/all_to_all | solution.py:194

commit v2 on v1

v2 whole, which is shorter than its diff:
```python
import math

import jax
import jax.numpy as jnp
import numpy as np
from jax import lax
from jax.experimental import pallas as pl
from jax.experimental.pallas import tpu as pltpu
from jax.sharding import PartitionSpec as P

AVG = 16
LANES = 128
BLOCK = 256
INNER = 256
F32 = jnp.float32
BF16 = jnp.bfloat16


def transform_tables(channels, n_freq, n_stn):
    j0 = np.arange(INNER, dtype=np.float64)
    k1 = np.arange(AVG, dtype=np.float64)
    phase = 2 * np.pi * k1[:, None] * j0[None, :] / channels + np.pi * j0[None, :] / (2 * channels)
    phase = phase + np.pi * (2 * k1[:, None] + 1) / (4 * channels)
    twiddle = np.stack([np.cos(phase), -np.sin(phase)]).astype(np.float32)
    groups = channels // AVG
    per_device = groups // (n_freq * n_stn)
    k2 = np.arange(groups).reshape(n_freq, n_stn, per_device).transpose(1, 0, 2).reshape(-1)
    phase = 2 * np.pi * (k2[:, None] * np.arange(INNER)[None, :] % INNER) / INNER
    phase = phase + 2 * np.pi * AVG * k2[:, None] / (4 * channels)
    scale = math.sqrt(2.0 / channels)
    exact = np.concatenate([np.cos(phase), np.sin(phase)], axis=1) * scale
    exact = jnp.asarray(exact.astype(np.float32))
    high = exact.astype(BF16)
    low = (exact - high.astype(F32)).astype(BF16)
    return jnp.asarray(twiddle), jnp.concatenate([high, high, low], axis=1)


def times(value, angle):
    c, s = math.cos(angle), math.sin(angle)
    re, im = value
    return re * c + im * s, im * c - re * s


def four_point(u0, u1, u2, u3):
    def add(a, b):
        return a[0] + b[0], a[1] + b[1]

    def sub(a, b):
        return a[0] - b[0], a[1] - b[1]

    s0, s1, t0, t1 = add(u0, u2), sub(u0, u2), add(u1, u3), sub(u1, u3)
    return add(s0, t0), (s1[0] + t1[1], s1[1] - t1[0]), sub(s0, t0), (s1[0] - t1[1], s1[1] + t1[0])


def sixteen_point(x):
    mid = []
    for b in range(4):
        u = [(x[b], jnp.zeros_like(x[b]))]
        for a in range(1, 4):
            angle = math.pi * a / 8
            u.append((x[4 * a + b] * math.cos(angle), x[4 * a + b] * -math.sin(angle)))
        row = four_point(*u)
        mid.append([times(row[p], 2 * math.pi * b * p / 16 + math.pi * b / 32) if b else row[p] for p in range(4)])
    y = [None] * 16
    for p in range(4):
        out = four_point(*[mid[b][p] for b in range(4)])
        for q in range(4):
            y[p + 4 * q] = out[q]
    return y


def channelize_kernel(x_ref, taps_ref, twiddle_ref, second_ref, keep_ref, out_ref, window, stage, turned):
    sources, signals, per_source, channels = x_ref.shape
    taps = taps_ref.shape[0]
    groups = second_ref.shape[0]
    rows = signals * per_source
    halves = INNER // LANES

    odd = lax.broadcasted_iota(jnp.int32, (rows, LANES), 0) % 2 == 1

    def fir(block, carry):
        lanes = pl.ds(pl.multiple_of(block * LANES, LANES), LANES)
        tap = [jnp.broadcast_to(taps_ref[pl.ds(t, 1), lanes], (rows, LANES)) for t in range(taps)]
        x = [x_ref[f, :, :, lanes].reshape(rows, LANES).astype(F32) for f in range(sources)]
        up = [pltpu.roll(v, rows - 1, 0) for v in x]
        down = [pltpu.roll(v, 1, 0) for v in x]
        late = [jnp.where(odd, down[f], up[f - 1] if f else 0.0) for f in range(sources)]
        for f in range(sources):
            total = tap[0] * x[f] + tap[1] * late[f]
            for u in range(1, min(taps // 2, f + 1)):
                total = total + tap[2 * u] * x[f - u] + tap[2 * u + 1] * late[f - u]
            window[f, :, lanes] = total
        return carry

    lax.fori_loop(0, channels // LANES, fir, 0)

    def first(f, carry):
        for half in range(halves):
            at = pl.ds(half * LANES, LANES)
            x = [window[f, :, pl.ds(j1 * INNER + half * LANES, LANES)] for j1 in range(AVG)]
            for k1, y in enumerate(sixteen_point(x)):
                tre = twiddle_ref[0, pl.ds(k1, 1), at]
                tim = twiddle_ref[1, pl.ds(k1, 1), at]
                to = pl.ds(pl.multiple_of((k1 * sources + f) * rows, rows), rows)
                stage[half, to, :] = y[0] * tre - y[1] * tim
                stage[halves + half, to, :] = y[0] * tim + y[1] * tre
        return carry

    lax.fori_loop(0, sources, first, 0)

    depth = AVG * sources
    columns = per_source * depth
    for s in range(signals):
        parts = [
            jnp.concatenate(
                [stage[part, pl.ds(s * per_source + i, depth, stride=rows), :] for part in range(2 * halves)], axis=1
            )
            for i in range(per_source)
        ]
        y = jnp.concatenate(parts, axis=0)
        high = y.astype(BF16)
        low = (y - high.astype(F32)).astype(BF16)
        z = lax.dot_general(
            second_ref[...],
            jnp.concatenate([high, low, high], axis=1),
            (((1,), (1,)), ((), ())),
            preferred_element_type=F32,
        )
        for c in range(columns // LANES):
            turned[c, pl.ds(s, groups, stride=signals), :] = z[:, c * LANES : (c + 1) * LANES]

    blocks = columns // LANES

    def last(step, carry):
        rows_in = pl.ds(pl.multiple_of(step * 32 * signals, 32 * signals), 32 * signals)
        to = pl.ds(pl.multiple_of(step * 16 * signals, 16 * signals), 16 * signals)
        for c in range(blocks):
            keep = keep_ref[c * per_source // blocks]
            value = turned[c, rows_in, :].reshape(16, 2, signals, LANES) * keep[None, None]
            for pair in range(2):
                part = value[:, pair].reshape(16 * signals, LANES).astype(BF16)
                out_ref[to, pair * columns + c * LANES : pair * columns + (c + 1) * LANES] = part
        return carry

    lax.fori_loop(0, groups // 32, last, 0)


def channelize(x, taps, twiddle, second, keep):
    sources, signals, per_source, channels = x.shape
    groups = channels // AVG
    columns = AVG * sources * per_source
    whole = pl.BlockSpec(memory_space=pltpu.VMEM)
    return pl.pallas_call(
        channelize_kernel,
        out_shape=jax.ShapeDtypeStruct((groups // 2 * signals, 2 * columns), BF16),
        in_specs=[whole] * 5,
        out_specs=whole,
        scratch_shapes=[
            pltpu.VMEM((sources, signals * per_source, channels), F32),
            pltpu.VMEM((4, AVG * sources * signals * per_source, LANES), F32),
            pltpu.VMEM((columns // LANES, groups * signals, LANES), F32),
        ],
        compiler_params=pltpu.CompilerParams(vmem_limit_bytes=28 * 1024 * 1024),
        name="channelize",
    )(x, taps, twiddle, second, keep)


def correlate_kernel(data_ref, out_ref):
    signals, width = data_ref.shape
    n_stn, pairs, rows, _ = out_ref.shape
    columns = width // pairs
    for pair in range(pairs):
        at = slice(pair * columns, (pair + 1) * columns)

        def block(c, carry):
            others = pl.ds(pl.multiple_of(c * BLOCK, BLOCK), BLOCK)
            sums = lax.dot_general(
                data_ref[:, at], data_ref[others, at], (((1,), (1,)), ((), ())), preferred_element_type=F32
            ).astype(BF16)
            out_ref[:, pair, :, others] = sums.reshape(n_stn, rows, BLOCK)
            return carry

        lax.fori_loop(0, signals // BLOCK, block, 0)


def correlate(data, n_stn):
    signals, width = data.shape
    whole = pl.BlockSpec(memory_space=pltpu.VMEM)
    return pl.pallas_call(
        correlate_kernel,
        out_shape=jax.ShapeDtypeStruct((n_stn, 2, signals // n_stn, signals), BF16),
        in_specs=[whole],
        out_specs=whole,
        compiler_params=pltpu.CompilerParams(vmem_limit_bytes=16 * 1024 * 1024),
        name="correlate",
    )(data)


def scale_kernel(sums_ref, scale_ref, out_ref):
    out_ref[...] = sums_ref[pl.program_id(0)].astype(F32)[None] * scale_ref[...]


def scaled(sums, scale):
    n, rows, signals = sums.shape
    whole = pl.BlockSpec(memory_space=pltpu.VMEM)
    return pl.pallas_call(
        scale_kernel,
        out_shape=jax.ShapeDtypeStruct((n, rows, signals), F32),
        grid=(n,),
        in_specs=[whole, whole],
        out_specs=pl.BlockSpec((1, rows, signals), lambda d: (d, 0, 0)),
        compiler_params=pltpu.CompilerParams(vmem_limit_bytes=16 * 1024 * 1024),
        name="scaled",
    )(sums, scale)


def body(voltages, filter_taps, station_flags):
    sig_dev, spec_dev, channels = voltages.shape
    n_freq, n_stn = lax.axis_size("freq"), lax.axis_size("stn")
    own = sig_dev // n_freq
    flags = jnp.repeat(station_flags, 2, axis=0).astype(F32)
    at_freq, at_stn = lax.axis_index("freq"), lax.axis_index("stn")
    keep = lax.dynamic_slice_in_dim(flags, at_stn * sig_dev + at_freq * own, own, 0)
    keep = keep.reshape(own, n_freq, spec_dev).transpose(2, 0, 1)
    keep = jnp.tile(keep, (1, 1, LANES // n_freq))
    twiddle, second = transform_tables(channels, n_freq, n_stn)

    x = lax.all_to_all(voltages.reshape(n_freq, own, spec_dev, channels), "freq", split_axis=0, concat_axis=0, tiled=True)
    kept = channelize(x, filter_taps, twiddle, second, keep)
    data = lax.all_to_all(kept, ("stn", "freq"), split_axis=0, concat_axis=0, tiled=True)
    sums = correlate(data, n_stn)
    sums = lax.all_to_all(sums, "stn", split_axis=0, concat_axis=0, tiled=True)
    own_flags = lax.dynamic_slice_in_dim(flags, at_stn * sig_dev, sig_dev, 0)
    counts = jnp.dot(own_flags, flags.T, precision=lax.Precision.HIGHEST)
    scale = 1.0 / (AVG * jnp.maximum(counts, 1.0))
    return scaled(sums.reshape(n_stn * 2, sig_dev, -1), scale)


def solution(mesh):
    in_specs = (P("stn", "freq", None), P(), P())
    out_specs = P("freq", "stn", None)
    return jax.shard_map(body, mesh=mesh, in_specs=in_specs, out_specs=out_specs, check_vma=False)
```

time: 165 us -> 161 us (0.976)
  Pallas kernels: 21.3 us -> 28.2 us
  other arithmetic: 6.8 us -> 0.01 us
  local copies, waits for them, and re-layouts: 6.81 us -> 3.38 us
    pallas_call x0 -> x1, Pallas kernels: none -> 9.04 us  [scaled(): pl.pallas_call(scale_kernel, out_shape=jax.ShapeDtypeStruct((n, rows, sig...]
    mul x1 -> x0, other arithmetic: 6.8 us -> none  [body(): return sums.reshape(n_stn * 2, sig_dev, -1).astype(F32) * scale[None]]
    reshape x1 -> x0, local copies, waits for them, and re-layouts: 4.29 us -> none  [body(): voltages.reshape(n_freq, own, spec_dev, channels)]
    pallas_call x1, Pallas kernels: 7.45 us -> 3.77 us  [correlate(): pl.pallas_call(correlate_kernel, out_shape=jax.ShapeDtypeStruct((n_stn, 2...]
where the time goes in v2:
time: 161 us
  waiting for transfers between devices  75.1 us (47%)
  blocking collectives  40.5 us (25%)
  Pallas kernels  28.2 us (18%)
  starting transfers between devices  13.3 us (8%)
  local copies, waits for them, and re-layouts  3.38 us (2%)
    all_to_all x1, waiting for transfers between devices, body(): sums = lax.all_to_all(sums, 'stn', split_axis=0, concat_axis=0, tiled=True)  48 us
    all_to_all x1, blocking collectives, body(): lax.all_to_all(kept, ('stn', 'freq'), split_axis=0, concat_axis=0, tiled=...  40.5 us
    all_to_all x1, waiting for transfers between devices, body(): lax.all_to_all(voltages.reshape(n_freq, own, spec_dev, channels), 'freq',...  27.1 us
    pallas_call x1, Pallas kernels, channelize(): pl.pallas_call(channelize_kernel, out_shape=jax.ShapeDtypeStruct((groups...  15.4 us
    pallas_call x1, Pallas kernels, scaled(): pl.pallas_call(scale_kernel, out_shape=jax.ShapeDtypeStruct((n, rows, sig...  9.04 us
    all_to_all x1, starting transfers between devices, body(): lax.all_to_all(voltages.reshape(n_freq, own, spec_dev, channels), 'freq',...  8.59 us
    all_to_all x1, starting transfers between devices, body(): sums = lax.all_to_all(sums, 'stn', split_axis=0, concat_axis=0, tiled=True)  4.68 us
    pallas_call x1, Pallas kernels, correlate(): pl.pallas_call(correlate_kernel, out_shape=jax.ShapeDtypeStruct((n_stn, 2...  3.77 us
  transfers between devices with their start and end apart: 2, of which 2 were waited for; matrix products, arithmetic and copies ran while one was open for 1% of the time, Pallas kernels for 0%

profile of v2, /device:TPU:1, one launch (start us, length us, event | category | flops | bytes accessed | tf_op | source)
XLA Modules:
  0.0 161.1 jit_solution(1395109599723998096)
XLA Ops:
  0.0 0.0 copy-start.6
  0.0 0.0 copy-start.1
  0.0 0.0 copy-start.2
  0.0 0.0 copy-start.3
  0.0 8.6 %all-to-all-start = ((bf16[16,8,2,4096]{3,2,1,0:T(2,128)(2,1)}), bf16[16,8,2,4096]{3,2,1,0:T(2,128)(2,1)S(1)}, u32[]{:S(2)}, u32[]{:S(2)}) async-start(bf16[16,8,2,4096]{3,2,1,0:T(2,128)(2,1)} %bitcast.13), calls=%async_computation | async-start | bytes 4194304 | tf_op jit(solution)/shard_map/all_to_all | solution.py:228
  8.6 0.0 copy-done.6
  8.6 0.1 copy.8
  8.8 0.2 broadcast_in_dim.3
  9.0 0.0 copy-start.4
  9.0 0.8 copy-done.4
  9.8 0.1 copy.9
  9.8 0.1 copy.10
  9.9 0.1 tile.10.keep_ref
  10.0 27.1 %all-to-all-done.x_ref = bf16[16,8,2,4096]{3,2,1,0:T(2,128)(2,1)S(1)} async-done(((bf16[16,8,2,4096]{3,2,1,0:T(2,128)(2,1)}), bf16[16,8,2,4096]{3,2,1,0:T(2,128)(2,1)S(1)}, u32[]{:S(2)}, u32[]{:S(2)}) %all-to-all-start) | async-done | bytes 2097184 | tf_op jit(solution)/shard_map/all_to_all | solution.py:228
  37.1 0.0 copy-done.1
  37.1 0.0 copy-done.2
  37.1 0.0 copy-done.3
  37.1 15.4 %channelize.1 = bf16[1024,1024]{1,0:T(8,128)(2,1)S(1)} custom-call(bf16[16,8,2,4096]{3,2,1,0:T(2,128)(2,1)S(1)} %all-to-all-done.x_ref, f32[16,4096]{1,0:T(8,128)S(1)} %copy-done.2, f32[2,16,256]{2,1,0:T(8,128)S(1)} %copy-done.3, bf16[256,1536]{1,0:T(8,128)(2,1)S(1)} %copy-done.1, f32[2,8,128]{2,1,0:T(8,128)S(1)} %tile.10.keep_ref), custom_call_target="tpu_custom_call" | custom-call | tf_op jit(solution)/shard_map/channelize/pallas_call | solution.py:153
  52.5 40.5 %all_to_all.21 = bf16[128,8,1024]{2,1,0:T(8,128)(2,1)S(1)} all-to-all(bf16[128,8,1024]{2,1,0:T(8,128)(2,1)S(1)} %bitcast.11), channel_id=1, replica_groups=mesh['freq'=16,'stn'=8] {'stn','freq'}, dimensions={0} | all-to-all | bytes 4194304 | tf_op jit(solution)/shard_map/all_to_all | solution.py:230
  93.0 3.8 %correlate.1 = bf16[8,2,128,1024]{3,2,1,0:T(8,128)(2,1)S(1)} custom-call(bf16[1024,1024]{1,0:T(8,128)(2,1)S(1)} %bitcast.12), custom_call_target="tpu_custom_call" | custom-call | tf_op jit(solution)/shard_map/correlate/pallas_call | solution.py:189
  96.7 0.0 copy-start
  96.7 2.0 %copy-done = bf16[8,2,128,1024]{3,2,1,0:T(8,128)(2,1)} copy-done((bf16[8,2,128,1024]{3,2,1,0:T(8,128)(2,1)}, bf16[8,2,128,1024]{3,2,1,0:T(8,128)(2,1)S(1)}, u32[]{:S(2)}) %copy-start) | copy-done | bytes 4194328
  98.8 0.0 copy-start.5
  98.8 4.7 %all-to-all-start.2 = ((bf16[8,2,128,1024]{3,2,1,0:T(8,128)(2,1)}), bf16[8,2,128,1024]{3,2,1,0:T(8,128)(2,1)}, u32[]{:S(2)}, u32[]{:S(2)}) async-start(bf16[8,2,128,1024]{3,2,1,0:T(8,128)(2,1)} %copy-done), calls=%async_computation.2 | async-start | bytes 8388608 | tf_op jit(solution)/shard_map/all_to_all | solution.py:232
  103.4 0.0 copy-done.5
  103.5 0.6 fusion.1.scale_ref
  104.1 48.0 %all-to-all-done.2 = bf16[8,2,128,1024]{3,2,1,0:T(8,128)(2,1)} async-done(((bf16[8,2,128,1024]{3,2,1,0:T(8,128)(2,1)}), bf16[8,2,128,1024]{3,2,1,0:T(8,128)(2,1)}, u32[]{:S(2)}, u32[]{:S(2)}) %all-to-all-start.2) | async-done | bytes 4194336 | tf_op jit(solution)/shard_map/all_to_all | solution.py:232
  152.1 9.0 %scaled.1 = f32[16,128,1024]{2,1,0:T(8,128)} custom-call(bf16[16,128,1024]{2,1,0:T(8,128)(2,1)} %bitcast.6.sums_ref, f32[128,1024]{1,0:T(8,128)S(1)} %fusion.1.scale_ref), custom_call_target="tpu_custom_call" | custom-call | tf_op jit(solution)/shard_map/scaled/pallas_call | solution.py:206
  (3 shorter events, 0.0 us)
Async XLA Ops:
  0.0 8.6 %copy-start.6 = (s32[512,32]{0,1:T(8,128)S(1)}, s32[512,32]{0,1:T(8,128)}, u32[]{:S(2)}) copy-start(s32[512,32]{0,1:T(8,128)} %param.7) | copy-start | bytes 196612
  0.0 37.1 %copy-start.1 = (bf16[256,1536]{1,0:T(8,128)(2,1)S(1)}, bf16[256,1536]{1,0:T(8,128)(2,1)}, u32[]{:S(2)}) copy-start(bf16[256,1536]{1,0:T(8,128)(2,1)} %constant.32.second_ref) | copy-start | bytes 2359300
  0.0 37.1 %copy-start.2 = (f32[16,4096]{1,0:T(8,128)S(1)}, f32[16,4096]{1,0:T(8,128)}, u32[]{:S(2)}) copy-start(f32[16,4096]{1,0:T(8,128)} %taps_ref.1) | copy-start | bytes 786436
  0.0 37.1 %copy-start.3 = (f32[2,16,256]{2,1,0:T(8,128)S(1)}, f32[2,16,256]{2,1,0:T(8,128)}, u32[]{:S(2)}) copy-start(f32[2,16,256]{2,1,0:T(8,128)} %constant.26.clone.twiddle_ref) | copy-start | bytes 98308
  0.0 37.1 %all-to-all-start = ((bf16[16,8,2,4096]{3,2,1,0:T(2,128)(2,1)}), bf16[16,8,2,4096]{3,2,1,0:T(2,128)(2,1)S(1)}, u32[]{:S(2)}, u32[]{:S(2)}) async-start(bf16[16,8,2,4096]{3,2,1,0:T(2,128)(2,1)} %bitcast.13), calls=%async_computation | async-start | bytes 4194304 | tf_op jit(solution)/shard_map/all_to_all | solution.py:228
  9.0 0.8 copy-start.4
  96.7 2.0 %copy-start = (bf16[8,2,128,1024]{3,2,1,0:T(8,128)(2,1)}, bf16[8,2,128,1024]{3,2,1,0:T(8,128)(2,1)S(1)}, u32[]{:S(2)}) copy-start(bf16[8,2,128,1024]{3,2,1,0:T(8,128)(2,1)S(1)} %correlate.1) | copy-start | bytes 12582916
  98.8 4.7 %copy-start.5 = (f32[512,2,32]{2,1,0:T(2,128)S(1)}, f32[512,2,32]{2,1,0:T(2,128)}, u32[]{:S(2)}) copy-start(f32[512,2,32]{2,1,0:T(2,128)} %copy-done.4) | copy-start | bytes 393220
  98.8 53.3 %all-to-all-start.2 = ((bf16[8,2,128,1024]{3,2,1,0:T(8,128)(2,1)}), bf16[8,2,128,1024]{3,2,1,0:T(8,128)(2,1)}, u32[]{:S(2)}, u32[]{:S(2)}) async-start(bf16[8,2,128,1024]{3,2,1,0:T(8,128)(2,1)} %copy-done), calls=%async_computation.2 | async-start | bytes 8388608 | tf_op jit(solution)/shard_map/all_to_all | solution.py:232

commit v3 on v2

v3 whole, which is shorter than its diff:
```python
import functools
import math

import jax
import jax.numpy as jnp
import numpy as np
from jax import lax
from jax.experimental import pallas as pl
from jax.experimental.pallas import tpu as pltpu
from jax.sharding import PartitionSpec as P

AVG = 16
LANES = 128
BLOCK = 256
TOGETHER = ((6,), (4,), (2,), (1,), (3,), (5,), (7,), (0,))
ARRIVING = ((0, 6), (4,), (2,), (1, 3, 5, 7))
INNER = 256
F32 = jnp.float32
BF16 = jnp.bfloat16


def transform_tables(channels, n_freq, n_stn):
    j0 = np.arange(INNER, dtype=np.float64)
    k1 = np.arange(AVG, dtype=np.float64)
    phase = 2 * np.pi * k1[:, None] * j0[None, :] / channels + np.pi * j0[None, :] / (2 * channels)
    phase = phase + np.pi * (2 * k1[:, None] + 1) / (4 * channels)
    twiddle = np.stack([np.cos(phase), -np.sin(phase)]).astype(np.float32)
    groups = channels // AVG
    per_device = groups // (n_freq * n_stn)
    k2 = np.arange(groups).reshape(n_freq, n_stn, per_device).transpose(1, 0, 2).reshape(-1)
    phase = 2 * np.pi * (k2[:, None] * np.arange(INNER)[None, :] % INNER) / INNER
    phase = phase + 2 * np.pi * AVG * k2[:, None] / (4 * channels)
    scale = math.sqrt(2.0 / channels)
    exact = np.concatenate([np.cos(phase), np.sin(phase)], axis=1) * scale
    exact = jnp.asarray(exact.astype(np.float32))
    high = exact.astype(BF16)
    low = (exact - high.astype(F32)).astype(BF16)
    twiddle, high, low = lax.optimization_barrier((jnp.asarray(twiddle), high, low))
    return jnp.stack([twiddle[0], twiddle[1]]), jnp.concatenate([high, high, low], axis=1)


def times(value, angle):
    c, s = math.cos(angle), math.sin(angle)
    re, im = value
    return re * c + im * s, im * c - re * s


def four_point(u0, u1, u2, u3):
    def add(a, b):
        return a[0] + b[0], a[1] + b[1]

    def sub(a, b):
        return a[0] - b[0], a[1] - b[1]

    s0, s1, t0, t1 = add(u0, u2), sub(u0, u2), add(u1, u3), sub(u1, u3)
    return add(s0, t0), (s1[0] + t1[1], s1[1] - t1[0]), sub(s0, t0), (s1[0] - t1[1], s1[1] + t1[0])


def sixteen_point(x):
    mid = []
    for b in range(4):
        u = [(x[b], jnp.zeros_like(x[b]))]
        for a in range(1, 4):
            angle = math.pi * a / 8
            u.append((x[4 * a + b] * math.cos(angle), x[4 * a + b] * -math.sin(angle)))
        row = four_point(*u)
        mid.append([times(row[p], 2 * math.pi * b * p / 16 + math.pi * b / 32) if b else row[p] for p in range(4)])
    y = [None] * 16
    for p in range(4):
        out = four_point(*[mid[b][p] for b in range(4)])
        for q in range(4):
            y[p + 4 * q] = out[q]
    return y


def channelize_kernel(
    x_ref, taps_hbm, keep_hbm, twiddle_hbm, second_hbm, out_hbm,
    window, stage_even, stage_odd, turned, out, taps_ref, keep_ref, twiddle_ref, second_ref, table_sems, out_sems,
):
    sources, signals, per_source, channels = x_ref.shape
    taps = taps_ref.shape[0]
    groups = second_ref.shape[0]
    frames = sources * per_source
    halves = INNER // LANES
    lane_blocks = channels // LANES
    chunk = 8 * LANES

    tables = [
        pltpu.make_async_copy(source, target, table_sems.at[n])
        for n, (source, target) in enumerate(
            ((taps_hbm, taps_ref), (keep_hbm, keep_ref), (twiddle_hbm, twiddle_ref), (second_hbm, second_ref))
        )
    ]
    for copy in tables:
        copy.start()
    tables[0].wait()

    def fir(step, carry):
        s = step // (channels // chunk)
        c = step % (channels // chunk)
        tap = [taps_ref[t, pl.ds(pl.multiple_of(c * 8, 8), 8), :] for t in range(taps)]
        x = []
        for f in range(sources):
            both = x_ref[f, s, :, pl.ds(pl.multiple_of(c * chunk, chunk), chunk)].astype(F32)
            for i in range(per_source):
                x.append(both[i : i + 1].reshape(8, LANES))
                m = f * per_source + i
                total, other = tap[0] * x[m], jnp.zeros((8, LANES), F32)
                for t in range(1, min(taps, m + 1)):
                    if t % 2:
                        other = other + tap[t] * x[m - t]
                    else:
                        total = total + tap[t] * x[m - t]
                window[pl.ds((s * frames + m) * (lane_blocks + 1) + c * 8, 8), :] = total + other
        return carry

    lax.fori_loop(0, signals * (channels // chunk), fir, 0)
    for copy in tables[1:]:
        copy.wait()

    columns = AVG * frames
    stages = (stage_even, stage_odd)

    def first(s):
        stage = stages[s % 2]
        for start in range(0, frames, 16):
            for half in range(halves):
                at = pl.ds(half * LANES, LANES)
                base = (s * frames + start) * (lane_blocks + 1) + half
                x = [window[pl.ds(base + j1 * halves, 16, stride=lane_blocks + 1), :] for j1 in range(AVG)]
                for k1, y in enumerate(sixteen_point(x)):
                    tre = twiddle_ref[0, pl.ds(k1, 1), at]
                    tim = twiddle_ref[1, pl.ds(k1, 1), at]
                    parts = (y[0] * tre - y[1] * tim, y[0] * tim + y[1] * tre)
                    for p, value in enumerate(parts):
                        high = value.astype(BF16)
                        low = (value - high.astype(F32)).astype(BF16)
                        to = pl.ds(k1 * frames + start, 16)
                        stage[to, pl.ds((p * halves + half) * LANES, LANES)] = high
                        stage[to, pl.ds((2 * halves + p * halves + half) * LANES, LANES)] = low

    def second(s):
        stage = stages[s % 2]
        width = 2 * INNER
        z = lax.dot_general(
            second_ref[...],
            jnp.concatenate([stage[...], stage[:, :width]], axis=1),
            (((1,), (1,)), ((), ())),
            preferred_element_type=F32,
        )
        for c in range(columns // LANES):
            turned[c, pl.ds(s, groups, stride=signals + 1), :] = z[:, c * LANES : (c + 1) * LANES]

    first(0)
    for s in range(signals):
        if s + 1 < signals:
            first(s + 1)
        second(s)

    keep = keep_ref[...]
    step_groups = 32
    step_rows = step_groups // 2 * signals

    def out_copy(step):
        rows = pl.ds(pl.multiple_of(step * step_rows, step_rows), step_rows)
        return pltpu.make_async_copy(out.at[rows, :], out_hbm.at[rows, :], out_sems.at[step])

    def last(step, carry):
        rows = pl.ds(pl.multiple_of(step * step_rows, step_rows), step_rows)
        for c in range(columns // LANES):
            for pair in range(2):
                value = jnp.concatenate(
                    [
                        turned[c, pl.ds((step * step_groups + g) * (signals + 1), signals), :] * keep
                        for g in range(pair, step_groups, 2)
                    ],
                    axis=0,
                )
                out[rows, pl.ds(pair * columns + c * LANES, LANES)] = value.astype(BF16)
        out_copy(step).start()
        return carry

    steps = groups // step_groups
    lax.fori_loop(0, steps, last, 0)
    for step in range(steps):
        out_copy(step).wait()


def channelize(x, taps, keep, twiddle, second):
    sources, signals, per_source, channels = x.shape
    groups = channels // AVG
    frames = sources * per_source
    columns = AVG * frames
    lane_blocks = channels // LANES
    whole = pl.BlockSpec(memory_space=pltpu.VMEM)
    hbm = pl.BlockSpec(memory_space=pltpu.HBM)
    shape = (groups // 2 * signals, 2 * columns)
    return pl.pallas_call(
        channelize_kernel,
        out_shape=jax.ShapeDtypeStruct(shape, BF16),
        in_specs=[whole] + [hbm] * 4,
        out_specs=hbm,
        scratch_shapes=[
            pltpu.VMEM((signals * frames * (lane_blocks + 1), LANES), F32),
            pltpu.VMEM((columns, 4 * INNER), BF16),
            pltpu.VMEM((columns, 4 * INNER), BF16),
            pltpu.VMEM((columns // LANES, groups * (signals + 1), LANES), F32),
            pltpu.VMEM(shape, BF16),
            pltpu.VMEM((taps.shape[0], lane_blocks, LANES), F32),
            pltpu.VMEM(keep.shape, F32),
            pltpu.VMEM(twiddle.shape, F32),
            pltpu.VMEM(second.shape, BF16),
            pltpu.SemaphoreType.DMA((4,)),
            pltpu.SemaphoreType.DMA((groups // 32,)),
        ],
        compiler_params=pltpu.CompilerParams(vmem_limit_bytes=28 * 1024 * 1024),
        name="channelize",
    )(x, taps.reshape(taps.shape[0], lane_blocks, LANES), keep, twiddle, second)


def correlate_kernel(to_ref, data_ref, *out_refs):
    pairs, rows, signals = out_refs[0].shape
    columns = data_ref.shape[1] // pairs
    for pair in range(pairs):
        at = slice(pair * columns, (pair + 1) * columns)
        own = [data_ref[pl.ds(pl.multiple_of(to_ref[n] * rows, rows), rows), at] for n in range(len(out_refs))]
        own = jnp.concatenate(own, axis=0)
        for c in range(signals // BLOCK):
            others = slice(c * BLOCK, (c + 1) * BLOCK)
            sums = lax.dot_general(own, data_ref[others, at], (((1,), (1,)), ((), ())), preferred_element_type=F32)
            for n, out_ref in enumerate(out_refs):
                out_ref[pair, :, others] = sums[n * rows : (n + 1) * rows].astype(BF16)


def correlate(data, to, n_stn):
    signals, width = data.shape
    rows = signals // n_stn
    whole = pl.BlockSpec(memory_space=pltpu.VMEM)
    return pl.pallas_call(
        correlate_kernel,
        out_shape=(jax.ShapeDtypeStruct((2, rows, signals), BF16),) * len(to),
        in_specs=[pl.BlockSpec(memory_space=pltpu.SMEM), whole],
        out_specs=(whole,) * len(to),
        compiler_params=pltpu.CompilerParams(vmem_limit_bytes=16 * 1024 * 1024),
        cost_estimate=pl.CostEstimate(
            flops=2 * len(to) * rows * signals * width, bytes_accessed=2 * signals * width, transcendentals=0
        ),
        name="correlate",
    )(jnp.stack(to).astype(jnp.int32), data)


def scale_kernel(at_ref, scale_ref, *refs):
    *tiles, out_ref = refs
    count = at_ref.shape[0]
    for n in range(count):

        @pl.when(pl.program_id(0) == n)
        def _():
            out_ref[...] = tiles[n][...].astype(F32) * scale_ref[...][None]


def scaled(tiles, scale, at, n_stn, buffer):
    pairs, rows, signals = tiles[0].shape
    extra = [] if buffer is None else [buffer]
    count = len(tiles)
    whole = pl.BlockSpec(memory_space=pltpu.VMEM)
    return pl.pallas_call(
        lambda at_ref, scale_ref, *refs: scale_kernel(at_ref, scale_ref, *refs[:count], refs[-1]),
        out_shape=jax.ShapeDtypeStruct((pairs * n_stn, rows, signals), F32),
        grid_spec=pltpu.PrefetchScalarGridSpec(
            num_scalar_prefetch=1,
            grid=(count, pairs),
            in_specs=[whole]
            + [pl.BlockSpec((1, rows, signals), functools.partial(tile_block, n, pairs)) for n in range(count)]
            + [pl.BlockSpec(memory_space=pl.ANY)] * len(extra),
            out_specs=pl.BlockSpec((1, rows, signals), lambda t, g, at: (pairs * at[t] + g, 0, 0)),
        ),
        input_output_aliases={2 + count: 0} if extra else {},
        compiler_params=pltpu.CompilerParams(vmem_limit_bytes=16 * 1024 * 1024),
        cost_estimate=pl.CostEstimate(
            flops=count * pairs * rows * signals, bytes_accessed=8 * count * pairs * rows * signals, transcendentals=0
        ),
        name="scaled",
    )(jnp.stack(at).astype(jnp.int32), scale, *tiles, *extra)


def tile_block(n, pairs, tile, pair, at_ref):
    return jnp.where(tile < n, 0, jnp.where(tile > n, pairs - 1, pair)), 0, 0


def body(voltages, filter_taps, station_flags):
    sig_dev, spec_dev, channels = voltages.shape
    n_freq, n_stn = lax.axis_size("freq"), lax.axis_size("stn")
    own = sig_dev // n_freq
    flags = jnp.repeat(station_flags, 2, axis=0).astype(F32)
    at_freq, at_stn = lax.axis_index("freq"), lax.axis_index("stn")
    keep = lax.dynamic_slice_in_dim(flags, at_stn * sig_dev + at_freq * own, own, 0)
    keep = jnp.tile(keep, (1, LANES // keep.shape[1]))
    twiddle, second = transform_tables(channels, n_freq, n_stn)

    x = lax.all_to_all(voltages.reshape(n_freq, own, spec_dev, channels), "freq", split_axis=0, concat_axis=0, tiled=True)
    kept = channelize(x, filter_taps, keep, twiddle, second)
    own_flags = lax.dynamic_slice_in_dim(flags, at_stn * sig_dev, sig_dev, 0)
    counts = jnp.dot(own_flags, flags.T, precision=lax.Precision.HIGHEST)
    scale = 1.0 / (AVG * jnp.maximum(counts, 1.0))
    partners = [at_stn ^ d for d in range(n_stn)]
    kept, scale, *partners = lax.optimization_barrier((kept, scale, *partners))
    data = lax.all_to_all(kept, ("stn", "freq"), split_axis=0, concat_axis=0, tiled=True)
    sent = {}
    for distances in TOGETHER:
        for distance, tile in zip(distances, correlate(data, [partners[d] for d in distances], n_stn)):
            route = [(i, i ^ distance) for i in range(n_stn)]
            sent[distance] = lax.ppermute(tile, "stn", route) if distance else tile
    result = None
    for distances in ARRIVING:
        result = scaled([sent[d] for d in distances], scale, [partners[d] for d in distances], n_stn, result)
    return result


def solution(mesh):
    in_specs = (P("stn", "freq", None), P(), P())
    out_specs = P("freq", "stn", None)
    return jax.shard_map(body, mesh=mesh, in_specs=in_specs, out_specs=out_specs, check_vma=False)
```

time: 161 us -> 146 us (0.907)
  waiting for transfers between devices: 75.1 us -> 58.7 us
    all_to_all x1 -> x0, waiting for transfers between devices: 48 us -> none  [body(): sums = lax.all_to_all(sums, 'stn', split_axis=0, concat_axis=0, tiled=True)]
    ppermute x0 -> x7, waiting for transfers between devices: none -> 33.3 us  [body(): sent[distance] = lax.ppermute(tile, 'stn', route) if distance else tile]
    ppermute x0 -> x7, starting transfers between devices: none -> 6.36 us  [body(): sent[distance] = lax.ppermute(tile, 'stn', route) if distance else tile]
    all_to_all x1 -> x0, starting transfers between devices: 4.68 us -> none  [body(): sums = lax.all_to_all(sums, 'stn', split_axis=0, concat_axis=0, tiled=True)]
    all_to_all x1, waiting for transfers between devices: 27.1 us -> 25.5 us  [body(): lax.all_to_all(voltages.reshape(n_freq, own, spec_dev, channels), 'freq',...]
    pallas_call x3 -> x13, Pallas kernels: 28.2 us -> 27.8 us  [the longest x1 12.6 us: channelize(): pl.pallas_call(channelize_kernel, out_shape=jax.ShapeDtypeStruct(shape, B...]
  transfers between devices with their start and end apart: 2 -> 8, of which waited for: 2 -> 6; matrix products, arithmetic and copies ran while one was open for 1% -> 2% of each run, Pallas kernels for 0% -> 7%
where the time goes in v3:
time: 146 us
  waiting for transfers between devices  58.7 us (40%)
  blocking collectives  40.5 us (28%)
  Pallas kernels  27.8 us (19%)
  starting transfers between devices  14.9 us (10%)
  local copies, waits for them, and re-layouts  2.12 us (1%)
    all_to_all x1, blocking collectives, body(): lax.all_to_all(kept, ('stn', 'freq'), split_axis=0, concat_axis=0, tiled=...  40.5 us
    ppermute x7, waiting for transfers between devices, body(): sent[distance] = lax.ppermute(tile, 'stn', route) if distance else tile  33.3 us
    all_to_all x1, waiting for transfers between devices, body(): lax.all_to_all(voltages.reshape(n_freq, own, spec_dev, channels), 'freq',...  25.5 us
    pallas_call x1, Pallas kernels, channelize(): pl.pallas_call(channelize_kernel, out_shape=jax.ShapeDtypeStruct(shape, B...  12.6 us
    pallas_call x4, Pallas kernels, scaled(): pl.pallas_call(lambda at_ref, scale_ref, *refs: scale_kernel(at_ref, scal...  8.59 us
    all_to_all x1, starting transfers between devices, body(): lax.all_to_all(voltages.reshape(n_freq, own, spec_dev, channels), 'freq',...  8.58 us
    pallas_call x8, Pallas kernels, correlate(): pl.pallas_call(correlate_kernel, out_shape=(jax.ShapeDtypeStruct((2, rows...  6.57 us
    ppermute x7, starting transfers between devices, body(): sent[distance] = lax.ppermute(tile, 'stn', route) if distance else tile  6.36 us
  transfers between devices with their start and end apart: 8, of which 6 were waited for; matrix products, arithmetic and copies ran while one was open for 2% of the time, Pallas kernels for 7%

profile of v3, /device:TPU:1, one launch (start us, length us, event | category | flops | bytes accessed | tf_op | source)
XLA Modules:
  0.0 146.1 jit_solution(16950928269370602064)
XLA Ops:
  0.0 8.6 %all-to-all-start = ((bf16[16,8,2,4096]{3,2,1,0:T(2,128)(2,1)}), bf16[16,8,2,4096]{3,2,1,0:T(2,128)(2,1)S(1)}, u32[]{:S(2)}, u32[]{:S(2)}) async-start(bf16[16,8,2,4096]{3,2,1,0:T(2,128)(2,1)} %bitcast.25), calls=%async_computation | async-start | bytes 4194304 | tf_op jit(solution)/shard_map/all_to_all | solution.py:301
  8.7 0.2 broadcast_in_dim.3
  9.1 0.8 copy.10
  9.8 0.6 fusion.1.scale_ref
  10.4 1.2 pad_maximum_fusion.second_hbm
  11.6 25.5 %all-to-all-done.x_ref = bf16[16,8,2,4096]{3,2,1,0:T(2,128)(2,1)S(1)} async-done(((bf16[16,8,2,4096]{3,2,1,0:T(2,128)(2,1)}), bf16[16,8,2,4096]{3,2,1,0:T(2,128)(2,1)S(1)}, u32[]{:S(2)}, u32[]{:S(2)}) %all-to-all-start) | async-done | bytes 2097184 | tf_op jit(solution)/shard_map/all_to_all | solution.py:301
  37.1 0.9 copy-done
  38.0 12.6 %channelize.1 = bf16[1024,1024]{1,0:T(8,128)(2,1)S(1)} custom-call(bf16[16,8,2,4096]{3,2,1,0:T(2,128)(2,1)S(1)} %all-to-all-done.x_ref, f32[16,32,128]{2,1,0:T(8,128)S(1)} %bitcast.24, f32[8,128]{1,0:T(8,128)S(1)} %tile.10.keep_hbm, f32[2,16,256]{2,1,0:T(8,128)S(1)} %copy-done.1, bf16[256,1536]{1,0:T(8,128)(2,1)S(1)} %pad_maximum_fusion.second_hbm), custom_call_target="tpu_custom_call" | custom-call | tf_op jit(solution)/shard_map/channelize/pallas_call | solution.py:198
  50.6 40.5 %all_to_all.16 = bf16[128,8,1024]{2,1,0:T(8,128)(2,1)S(1)} all-to-all(bf16[128,8,1024]{2,1,0:T(8,128)(2,1)S(1)} %bitcast.23), channel_id=1, replica_groups=mesh['freq'=16,'stn'=8] {'stn','freq'}, dimensions={0} | all-to-all | bytes 4194304 | tf_op jit(solution)/shard_map/all_to_all | solution.py:308
  91.1 0.8 correlate.15
  92.0 0.2 collective-permute-start.6
  92.1 0.8 correlate.13
  93.0 1.3 collective-permute-start.5
  94.3 0.8 correlate.12
  95.1 3.1 %collective-permute-start.4 = (bf16[2,128,1024]{2,1,0:T(8,128)(2,1)S(1)}, bf16[2,128,1024]{2,1,0:T(8,128)(2,1)S(1)}, u32[]{:S(2)}, u32[]{:S(2)}) collective-permute-start(bf16[2,128,1024]{2,1,0:T(8,128)(2,1)S(1)} %correlate.12), channel_id=1, source_target_pairs={{0,2},{1,3},{2,0},{3,1},{4,6},{5,7},{6,4},{7,5},{8,10},{9,11},{10,... | collective-permute-start | bytes 1572872 | tf_op jit(solution)/shard_map/ppermute | solution.py:313
  98.2 0.8 correlate.11
  99.0 0.4 collective-permute-start.3
  99.5 0.8 correlate.10
  100.3 0.5 collective-permute-start.2
  100.8 0.8 correlate.9
  101.6 0.8 correlate.8
  102.4 4.8 %collective-permute-done.6.refs_1_ = bf16[2,128,1024]{2,1,0:T(8,128)(2,1)S(1)} collective-permute-done((bf16[2,128,1024]{2,1,0:T(8,128)(2,1)S(1)}, bf16[2,128,1024]{2,1,0:T(8,128)(2,1)S(1)}, u32[]{:S(2)}, u32[]{:S(2)}) %collective-permute-start.6) | collective-permute-done | bytes 524320 | tf_op jit(solution)/shard_map/ppermute | solution.py:313
  107.3 8.3 %collective-permute-done.5.refs_0_ = bf16[2,128,1024]{2,1,0:T(8,128)(2,1)S(1)} collective-permute-done((bf16[2,128,1024]{2,1,0:T(8,128)(2,1)S(1)}, bf16[2,128,1024]{2,1,0:T(8,128)(2,1)S(1)}, u32[]{:S(2)}, u32[]{:S(2)}) %collective-permute-start.5) | collective-permute-done | bytes 524320 | tf_op jit(solution)/shard_map/ppermute | solution.py:313
  115.6 0.8 collective-permute-start
  116.5 0.8 correlate.14.refs_0_
  117.3 2.4 %scaled.4.refs_1_ = f32[16,128,1024]{2,1,0:T(8,128)} custom-call(s32[2]{0:T(128)S(1)} %pad_add_fusion.1.at_ref, f32[128,1024]{1,0:T(8,128)S(1)} %fusion.1.scale_ref, bf16[2,128,1024]{2,1,0:T(8,128)(2,1)S(1)} %correlate.14.refs_0_, bf16[2,128,1024]{2,1,0:T(8,128)(2,1)S(1)} %collective-permute-done.6.refs_1_), custom_call_target="tpu_custom_call" | custom-call | flops 524288 | bytes 4194304 | tf_op jit(solution)/shard_map/scaled/pallas_call | solution.py:267
  119.8 1.0 scaled.5.refs_1_
  120.8 1.0 scaled.6.refs_4_
  121.8 8.7 %collective-permute-done.3.refs_3_ = bf16[2,128,1024]{2,1,0:T(8,128)(2,1)S(1)} collective-permute-done((bf16[2,128,1024]{2,1,0:T(8,128)(2,1)S(1)}, bf16[2,128,1024]{2,1,0:T(8,128)(2,1)S(1)}, u32[]{:S(2)}, u32[]{:S(2)}) %collective-permute-start.3) | collective-permute-done | bytes 524320 | tf_op jit(solution)/shard_map/ppermute | solution.py:313
  130.5 8.5 %collective-permute-done.2.refs_2_ = bf16[2,128,1024]{2,1,0:T(8,128)(2,1)S(1)} collective-permute-done((bf16[2,128,1024]{2,1,0:T(8,128)(2,1)S(1)}, bf16[2,128,1024]{2,1,0:T(8,128)(2,1)S(1)}, u32[]{:S(2)}, u32[]{:S(2)}) %collective-permute-start.2) | collective-permute-done | bytes 524320 | tf_op jit(solution)/shard_map/ppermute | solution.py:313
  139.0 3.0 %collective-permute-done.1.refs_1_ = bf16[2,128,1024]{2,1,0:T(8,128)(2,1)S(1)} collective-permute-done((bf16[2,128,1024]{2,1,0:T(8,128)(2,1)S(1)}, bf16[2,128,1024]{2,1,0:T(8,128)(2,1)S(1)}, u32[]{:S(2)}, u32[]{:S(2)}) %collective-permute-start.1) | collective-permute-done | bytes 524320 | tf_op jit(solution)/shard_map/ppermute | solution.py:313
  142.0 4.1 %scaled.7 = f32[16,128,1024]{2,1,0:T(8,128)} custom-call(s32[4]{0:T(128)S(1)} %pad_add_fusion.at_ref, f32[128,1024]{1,0:T(8,128)S(1)} %fusion.1.scale_ref, bf16[2,128,1024]{2,1,0:T(8,128)(2,1)S(1)} %collective-permute-done.refs_0_, bf16[2,128,1024]{2,1,0:T(8,128)(2,1)S(1)} %collective-permute-done.1.refs_1_, ...), custom_call_target="tpu_custom_call", output_to_operand_aliasing={{}: (6, {})} | custom-call | flops 1048576 | bytes 8388608 | tf_op jit(solution)/shard_map/scaled/pallas_call | solution.py:267
  (17 shorter events, 0.5 us)
Async XLA Ops:
  0.0 8.6 %copy-start.3 = (s32[512,32]{0,1:T(8,128)S(1)}, s32[512,32]{0,1:T(8,128)}, u32[]{:S(2)}) copy-start(s32[512,32]{0,1:T(8,128)} %param.7) | copy-start | bytes 196612
  0.0 9.0 %copy-start.2 = (f32[16,4096]{1,0:T(8,128)S(1)}, f32[16,4096]{1,0:T(8,128)}, u32[]{:S(2)}) copy-start(f32[16,4096]{1,0:T(8,128)} %param.6) | copy-start | bytes 786436
  0.0 37.1 %all-to-all-start = ((bf16[16,8,2,4096]{3,2,1,0:T(2,128)(2,1)}), bf16[16,8,2,4096]{3,2,1,0:T(2,128)(2,1)S(1)}, u32[]{:S(2)}, u32[]{:S(2)}) async-start(bf16[16,8,2,4096]{3,2,1,0:T(2,128)(2,1)} %bitcast.25), calls=%async_computation | async-start | bytes 4194304 | tf_op jit(solution)/shard_map/all_to_all | solution.py:301
  8.9 28.1 %copy-start.1 = (f32[2,16,256]{2,1,0:T(8,128)S(1)}, f32[2,16,256]{2,1,0:T(8,128)}, u32[]{:S(2)}) copy-start(f32[2,16,256]{2,1,0:T(8,128)} %constant.40.clone.twiddle_hbm) | copy-start | bytes 98308
  37.1 1.0 copy-start
  92.0 15.2 %collective-permute-start.6 = (bf16[2,128,1024]{2,1,0:T(8,128)(2,1)S(1)}, bf16[2,128,1024]{2,1,0:T(8,128)(2,1)S(1)}, u32[]{:S(2)}, u32[]{:S(2)}) collective-permute-start(bf16[2,128,1024]{2,1,0:T(8,128)(2,1)S(1)} %correlate.15), channel_id=1, source_target_pairs={{0,6},{1,7},{2,4},{3,5},{4,2},{5,3},{6,0},{7,1},{8,14},{9,15},{10,... | collective-permute-start | bytes 1572872 | tf_op jit(solution)/shard_map/ppermute | solution.py:313
  93.0 22.6 %collective-permute-start.5 = (bf16[2,128,1024]{2,1,0:T(8,128)(2,1)S(1)}, bf16[2,128,1024]{2,1,0:T(8,128)(2,1)S(1)}, u32[]{:S(2)}, u32[]{:S(2)}) collective-permute-start(bf16[2,128,1024]{2,1,0:T(8,128)(2,1)S(1)} %correlate.13), channel_id=1, source_target_pairs={{0,4},{1,5},{2,6},{3,7},{4,0},{5,1},{6,2},{7,3},{8,12},{9,13},{10,... | collective-permute-start | bytes 1572872 | tf_op jit(solution)/shard_map/ppermute | solution.py:313
  95.1 25.7 %collective-permute-start.4 = (bf16[2,128,1024]{2,1,0:T(8,128)(2,1)S(1)}, bf16[2,128,1024]{2,1,0:T(8,128)(2,1)S(1)}, u32[]{:S(2)}, u32[]{:S(2)}) collective-permute-start(bf16[2,128,1024]{2,1,0:T(8,128)(2,1)S(1)} %correlate.12), channel_id=1, source_target_pairs={{0,2},{1,3},{2,0},{3,1},{4,6},{5,7},{6,4},{7,5},{8,10},{9,11},{10,... | collective-permute-start | bytes 1572872 | tf_op jit(solution)/shard_map/ppermute | solution.py:313
  99.0 31.5 %collective-permute-start.3 = (bf16[2,128,1024]{2,1,0:T(8,128)(2,1)S(1)}, bf16[2,128,1024]{2,1,0:T(8,128)(2,1)S(1)}, u32[]{:S(2)}, u32[]{:S(2)}) collective-permute-start(bf16[2,128,1024]{2,1,0:T(8,128)(2,1)S(1)} %correlate.11), channel_id=1, source_target_pairs={{0,7},{1,6},{2,5},{3,4},{4,3},{5,2},{6,1},{7,0},{8,15},{9,14},{10,... | collective-permute-start | bytes 1572872 | tf_op jit(solution)/shard_map/ppermute | solution.py:313
  100.3 38.7 %collective-permute-start.2 = (bf16[2,128,1024]{2,1,0:T(8,128)(2,1)S(1)}, bf16[2,128,1024]{2,1,0:T(8,128)(2,1)S(1)}, u32[]{:S(2)}, u32[]{:S(2)}) collective-permute-start(bf16[2,128,1024]{2,1,0:T(8,128)(2,1)S(1)} %correlate.10), channel_id=1, source_target_pairs={{0,5},{1,4},{2,7},{3,6},{4,1},{5,0},{6,3},{7,2},{8,13},{9,12},{10,... | collective-permute-start | bytes 1572872 | tf_op jit(solution)/shard_map/ppermute | solution.py:313
  107.2 34.8 %collective-permute-start.1 = (bf16[2,128,1024]{2,1,0:T(8,128)(2,1)S(1)}, bf16[2,128,1024]{2,1,0:T(8,128)(2,1)S(1)}, u32[]{:S(2)}, u32[]{:S(2)}) collective-permute-start(bf16[2,128,1024]{2,1,0:T(8,128)(2,1)S(1)} %correlate.9), channel_id=1, source_target_pairs={{0,3},{1,2},{2,1},{3,0},{4,7},{5,6},{6,5},{7,4},{8,11},{9,10},{10,... | collective-permute-start | bytes 1572872 | tf_op jit(solution)/shard_map/ppermute | solution.py:313
  115.6 26.4 %collective-permute-start = (bf16[2,128,1024]{2,1,0:T(8,128)(2,1)S(1)}, bf16[2,128,1024]{2,1,0:T(8,128)(2,1)S(1)}, u32[]{:S(2)}, u32[]{:S(2)}) collective-permute-start(bf16[2,128,1024]{2,1,0:T(8,128)(2,1)S(1)} %correlate.8), channel_id=1, source_target_pairs={{0,1},{1,0},{2,3},{3,2},{4,5},{5,4},{6,7},{7,6},{8,9},{9,8},{10,11... | collective-permute-start | bytes 1572872 | tf_op jit(solution)/shard_map/ppermute | solution.py:313

commit v4 on v3

--- a/solution.py
+++ b/solution.py
@@ -13,7 +13,7 @@
 LANES = 128
 BLOCK = 256
 TOGETHER = ((6,), (4,), (2,), (1,), (3,), (5,), (7,), (0,))
-ARRIVING = ((0, 6), (4,), (2,), (1, 3, 5, 7))
+ARRIVING = ((0, 6), (4,), (2,), (1,), (3, 5, 7))
 INNER = 256
 F32 = jnp.float32
 BF16 = jnp.bfloat16
@@ -36,7 +36,7 @@
     high = exact.astype(BF16)
     low = (exact - high.astype(F32)).astype(BF16)
     twiddle, high, low = lax.optimization_barrier((jnp.asarray(twiddle), high, low))
-    return jnp.stack([twiddle[0], twiddle[1]]), jnp.concatenate([high, high, low], axis=1)
+    return jnp.stack([twiddle[0], twiddle[1]]), jnp.concatenate([high, low], axis=0)
 
 
 def times(value, angle):
@@ -74,12 +74,12 @@
 
 
 def channelize_kernel(
-    x_ref, taps_hbm, keep_hbm, twiddle_hbm, second_hbm, out_hbm,
+    x_ref, rows_ref, keep_hbm, twiddle_hbm, second_hbm, out_hbm,
     window, stage_even, stage_odd, turned, out, taps_ref, keep_ref, twiddle_ref, second_ref, table_sems, out_sems,
 ):
     sources, signals, per_source, channels = x_ref.shape
     taps = taps_ref.shape[0]
-    groups = second_ref.shape[0]
+    groups = second_ref.shape[0] // 2
     frames = sources * per_source
     halves = INNER // LANES
     lane_blocks = channels // LANES
@@ -88,12 +88,14 @@
     tables = [
         pltpu.make_async_copy(source, target, table_sems.at[n])
         for n, (source, target) in enumerate(
-            ((taps_hbm, taps_ref), (keep_hbm, keep_ref), (twiddle_hbm, twiddle_ref), (second_hbm, second_ref))
+            ((keep_hbm, keep_ref), (twiddle_hbm, twiddle_ref), (second_hbm, second_ref))
         )
     ]
     for copy in tables:
         copy.start()
-    tables[0].wait()
+    for t in range(taps):
+        for c in range(channels // chunk):
+            taps_ref[t, c * 8 : (c + 1) * 8, :] = rows_ref[t : t + 1, c * chunk : (c + 1) * chunk].reshape(8, LANES)
 
     def fir(step, carry):
         s = step // (channels // chunk)
@@ -115,7 +117,7 @@
         return carry
 
     lax.fori_loop(0, signals * (channels // chunk), fir, 0)
-    for copy in tables[1:]:
+    for copy in tables:
         copy.wait()
 
     columns = AVG * frames
@@ -142,12 +144,10 @@
     def second(s):
         stage = stages[s % 2]
         width = 2 * INNER
-        z = lax.dot_general(
-            second_ref[...],
-            jnp.concatenate([stage[...], stage[:, :width]], axis=1),
-            (((1,), (1,)), ((), ())),
-            preferred_element_type=F32,
-        )
+        across = (((1,), (1,)), ((), ()))
+        z = lax.dot_general(second_ref[...], stage[:, :width], across, preferred_element_type=F32)
+        z = z[:groups] + z[groups:]
+        z = z + lax.dot_general(second_ref[:groups], stage[:, width:], across, preferred_element_type=F32)
         for c in range(columns // LANES):
             turned[c, pl.ds(s, groups, stride=signals + 1), :] = z[:, c * LANES : (c + 1) * LANES]
 
@@ -198,7 +198,7 @@
     return pl.pallas_call(
         channelize_kernel,
         out_shape=jax.ShapeDtypeStruct(shape, BF16),
-        in_specs=[whole] + [hbm] * 4,
+        in_specs=[whole] * 2 + [hbm] * 3,
         out_specs=hbm,
         scratch_shapes=[
             pltpu.VMEM((signals * frames * (lane_blocks + 1), LANES), F32),
@@ -210,12 +210,12 @@
             pltpu.VMEM(keep.shape, F32),
             pltpu.VMEM(twiddle.shape, F32),
             pltpu.VMEM(second.shape, BF16),
-            pltpu.SemaphoreType.DMA((4,)),
+            pltpu.SemaphoreType.DMA((3,)),
             pltpu.SemaphoreType.DMA((groups // 32,)),
         ],
         compiler_params=pltpu.CompilerParams(vmem_limit_bytes=28 * 1024 * 1024),
         name="channelize",
-    )(x, taps.reshape(taps.shape[0], lane_blocks, LANES), keep, twiddle, second)
+    )(x, taps, keep, twiddle, second)
 
 
 def correlate_kernel(to_ref, data_ref, *out_refs):
@@ -249,14 +249,26 @@
     )(jnp.stack(to).astype(jnp.int32), data)
 
 
-def scale_kernel(at_ref, scale_ref, *refs):
-    *tiles, out_ref = refs
-    count = at_ref.shape[0]
+PARTS = 2
+
+
+def scale_kernel(count, at_ref, scale_ref, *refs):
+    tiles, (out_hbm, made, sems) = refs[:count], refs[-3:]
+    _, pairs, rows, _ = made.shape
+    part_rows = rows // PARTS
+    copies = []
     for n in range(count):
-
-        @pl.when(pl.program_id(0) == n)
-        def _():
-            out_ref[...] = tiles[n][...].astype(F32) * scale_ref[...][None]
+        for pair in range(pairs):
+            for part in range(PARTS):
+                own = pl.ds(part * part_rows, part_rows)
+                made[n, pair, own, :] = tiles[n][pair, own, :].astype(F32) * scale_ref[own, :]
+                copy = pltpu.make_async_copy(
+                    made.at[n, pair, own, :], out_hbm.at[pairs * at_ref[n] + pair, own, :], sems.at[len(copies)]
+                )
+                copy.start()
+                copies.append(copy)
+    for copy in copies:
+        copy.wait()
 
 
 def scaled(tiles, scale, at, n_stn, buffer):
@@ -265,16 +277,16 @@
     count = len(tiles)
     whole = pl.BlockSpec(memory_space=pltpu.VMEM)
     return pl.pallas_call(
-        lambda at_ref, scale_ref, *refs: scale_kernel(at_ref, scale_ref, *refs[:count], refs[-1]),
+        functools.partial(scale_kernel, count),
         out_shape=jax.ShapeDtypeStruct((pairs * n_stn, rows, signals), F32),
-        grid_spec=pltpu.PrefetchScalarGridSpec(
-            num_scalar_prefetch=1,
-            grid=(count, pairs),
-            in_specs=[whole]
-            + [pl.BlockSpec((1, rows, signals), functools.partial(tile_block, n, pairs)) for n in range(count)]
-            + [pl.BlockSpec(memory_space=pl.ANY)] * len(extra),
-            out_specs=pl.BlockSpec((1, rows, signals), lambda t, g, at: (pairs * at[t] + g, 0, 0)),
-        ),
+        in_specs=[pl.BlockSpec(memory_space=pltpu.SMEM)]
+        + [whole] * (1 + count)
+        + [pl.BlockSpec(memory_space=pl.ANY)] * len(extra),
+        out_specs=pl.BlockSpec(memory_space=pl.ANY),
+        scratch_shapes=[
+            pltpu.VMEM((count, pairs, rows, signals), F32),
+            pltpu.SemaphoreType.DMA((count * pairs * PARTS,)),
+        ],
         input_output_aliases={2 + count: 0} if extra else {},
         compiler_params=pltpu.CompilerParams(vmem_limit_bytes=16 * 1024 * 1024),
         cost_estimate=pl.CostEstimate(
@@ -282,10 +294,6 @@
         ),
         name="scaled",
     )(jnp.stack(at).astype(jnp.int32), scale, *tiles, *extra)
-
-
-def tile_block(n, pairs, tile, pair, at_ref):
-    return jnp.where(tile < n, 0, jnp.where(tile > n, pairs - 1, pair)), 0, 0
 
 
 def body(voltages, filter_taps, station_flags):

time: 146 us -> 143 us (0.979)
  waiting for transfers between devices: 58.7 us -> 54.6 us
  starting transfers between devices: 14.9 us -> 16.6 us
  Pallas kernels: 27.8 us -> 26.2 us
    ppermute x7, waiting for transfers between devices: 33.3 us -> 31 us  [body(): sent[distance] = lax.ppermute(tile, 'stn', route) if distance else tile]
    all_to_all x1, waiting for transfers between devices: 25.5 us -> 23.6 us  [body(): lax.all_to_all(voltages.reshape(n_freq, own, spec_dev, channels), 'freq',...]
    ppermute x7, starting transfers between devices: 6.36 us -> 8 us  [body(): sent[distance] = lax.ppermute(tile, 'stn', route) if distance else tile]
    pallas_call x4 -> x5, Pallas kernels: 8.59 us -> 7.32 us  [scaled(): pl.pallas_call(functools.partial(scale_kernel, count), out_shape=jax.Shap...]
  transfers between devices with their start and end apart: 8 -> 8, of which waited for: 6 -> 6; matrix products, arithmetic and copies ran while one was open for 2% -> 3% of each run, Pallas kernels for 7% -> 8%
where the time goes in v4:
time: 143 us
  waiting for transfers between devices  54.6 us (38%)
  blocking collectives  40.5 us (28%)
  Pallas kernels  26.2 us (18%)
  starting transfers between devices  16.6 us (12%)
  other arithmetic  2.06 us (1%)
  matrix products  1.73 us (1%)
    all_to_all x1, blocking collectives, body(): lax.all_to_all(kept, ('stn', 'freq'), split_axis=0, concat_axis=0, tiled=...  40.5 us
    ppermute x7, waiting for transfers between devices, body(): sent[distance] = lax.ppermute(tile, 'stn', route) if distance else tile  31 us
    all_to_all x1, waiting for transfers between devices, body(): lax.all_to_all(voltages.reshape(n_freq, own, spec_dev, channels), 'freq',...  23.6 us
    pallas_call x1, Pallas kernels, channelize(): pl.pallas_call(channelize_kernel, out_shape=jax.ShapeDtypeStruct(shape, B...  12.3 us
    all_to_all x1, starting transfers between devices, body(): lax.all_to_all(voltages.reshape(n_freq, own, spec_dev, channels), 'freq',...  8.58 us
    ppermute x7, starting transfers between devices, body(): sent[distance] = lax.ppermute(tile, 'stn', route) if distance else tile  8 us
    pallas_call x5, Pallas kernels, scaled(): pl.pallas_call(functools.partial(scale_kernel, count), out_shape=jax.Shap...  7.32 us
    pallas_call x8, Pallas kernels, correlate(): pl.pallas_call(correlate_kernel, out_shape=(jax.ShapeDtypeStruct((2, rows...  6.56 us
  transfers between devices with their start and end apart: 8, of which 6 were waited for; matrix products, arithmetic and copies ran while one was open for 3% of the time, Pallas kernels for 8%

profile of v4, /device:TPU:1, one launch (start us, length us, event | category | flops | bytes accessed | tf_op | source)
XLA Modules:
  0.0 143.2 jit_solution(10645589786130001251)
XLA Ops:
  0.0 8.6 %all-to-all-start = ((bf16[16,8,2,4096]{3,2,1,0:T(2,128)(2,1)}), bf16[16,8,2,4096]{3,2,1,0:T(2,128)(2,1)S(1)}, u32[]{:S(2)}, u32[]{:S(2)}) async-start(bf16[16,8,2,4096]{3,2,1,0:T(2,128)(2,1)} %bitcast.22), calls=%async_computation | async-start | bytes 4194304 | tf_op jit(solution)/shard_map/all_to_all | solution.py:309
  8.6 0.8 convert_element_type.16
  9.6 0.2 broadcast_in_dim.3
  9.8 0.8 copy-done.2
  10.6 1.1 pad_maximum_fusion.second_hbm
  11.7 1.7 %fusion.1.scale_ref = f32[128,1024]{1,0:T(8,128)S(1)} fusion(f32[1024,32]{1,0:T(8,128)} %bitcast.24, s32[]{:T(128)S(6)} %select_n.7), kind=kOutput, calls=%fused_computation.2 | convolution fusion | flops 50724864 | bytes 1114116 | tf_op jit(solution)/shard_map/dot_general | solution.py:312
  13.4 23.6 %all-to-all-done.x_ref = bf16[16,8,2,4096]{3,2,1,0:T(2,128)(2,1)S(1)} async-done(((bf16[16,8,2,4096]{3,2,1,0:T(2,128)(2,1)}), bf16[16,8,2,4096]{3,2,1,0:T(2,128)(2,1)S(1)}, u32[]{:S(2)}, u32[]{:S(2)}) %all-to-all-start) | async-done | bytes 2097184 | tf_op jit(solution)/shard_map/all_to_all | solution.py:309
  37.1 12.3 %channelize.1 = bf16[1024,1024]{1,0:T(8,128)(2,1)S(1)} custom-call(bf16[16,8,2,4096]{3,2,1,0:T(2,128)(2,1)S(1)} %all-to-all-done.x_ref, f32[16,4096]{1,0:T(8,128)S(1)} %copy-done, f32[8,128]{1,0:T(8,128)S(1)} %tile.10.keep_hbm, f32[2,16,256]{2,1,0:T(8,128)S(1)} %copy-done.1, bf16[512,512]{1,0:T(8,128)(2,1)S(1)} %pad_maximum_fusion.second_hbm), custom_call_target="tpu_custom_call" | custom-call | tf_op jit(solution)/shard_map/channelize/pallas_call | solution.py:198
  49.3 40.5 %all_to_all.16 = bf16[128,8,1024]{2,1,0:T(8,128)(2,1)S(1)} all-to-all(bf16[128,8,1024]{2,1,0:T(8,128)(2,1)S(1)} %bitcast.21), channel_id=1, replica_groups=mesh['freq'=16,'stn'=8] {'stn','freq'}, dimensions={0} | all-to-all | bytes 4194304 | tf_op jit(solution)/shard_map/all_to_all | solution.py:316
  89.8 0.8 correlate.15
  90.8 0.8 correlate.13
  91.7 1.3 collective-permute-start.5
  93.0 0.8 correlate.12
  93.8 2.9 %collective-permute-start.4 = (bf16[2,128,1024]{2,1,0:T(8,128)(2,1)S(1)}, bf16[2,128,1024]{2,1,0:T(8,128)(2,1)S(1)}, u32[]{:S(2)}, u32[]{:S(2)}) collective-permute-start(bf16[2,128,1024]{2,1,0:T(8,128)(2,1)S(1)} %correlate.12), channel_id=1, source_target_pairs={{0,2},{1,3},{2,0},{3,1},{4,6},{5,7},{6,4},{7,5},{8,10},{9,11},{10,... | collective-permute-start | bytes 1572872 | tf_op jit(solution)/shard_map/ppermute | solution.py:321
  96.7 0.8 correlate.11
  97.5 0.3 collective-permute-start.3
  97.8 0.8 correlate.10
  98.6 0.4 collective-permute-start.2
  99.1 0.8 correlate.9
  99.9 0.8 correlate.8
  100.7 5.2 %collective-permute-done.6.refs_1_ = bf16[2,128,1024]{2,1,0:T(8,128)(2,1)S(1)} collective-permute-done((bf16[2,128,1024]{2,1,0:T(8,128)(2,1)S(1)}, bf16[2,128,1024]{2,1,0:T(8,128)(2,1)S(1)}, u32[]{:S(2)}, u32[]{:S(2)}) %collective-permute-start.6) | collective-permute-done | bytes 524320 | tf_op jit(solution)/shard_map/ppermute | solution.py:321
  105.9 8.4 %collective-permute-done.5.refs_0_ = bf16[2,128,1024]{2,1,0:T(8,128)(2,1)S(1)} collective-permute-done((bf16[2,128,1024]{2,1,0:T(8,128)(2,1)S(1)}, bf16[2,128,1024]{2,1,0:T(8,128)(2,1)S(1)}, u32[]{:S(2)}, u32[]{:S(2)}) %collective-permute-start.5) | collective-permute-done | bytes 524320 | tf_op jit(solution)/shard_map/ppermute | solution.py:321
  114.3 2.9 %collective-permute-start = (bf16[2,128,1024]{2,1,0:T(8,128)(2,1)S(1)}, bf16[2,128,1024]{2,1,0:T(8,128)(2,1)S(1)}, u32[]{:S(2)}, u32[]{:S(2)}) collective-permute-start(bf16[2,128,1024]{2,1,0:T(8,128)(2,1)S(1)} %correlate.8), channel_id=1, source_target_pairs={{0,3},{1,2},{2,1},{3,0},{4,7},{5,6},{6,5},{7,4},{8,11},{9,10},{10,... | collective-permute-start | bytes 1572872 | tf_op jit(solution)/shard_map/ppermute | solution.py:321
  117.2 0.8 correlate.14.refs_0_
  118.0 2.0 %scaled.5.refs_1_ = f32[16,128,1024]{2,1,0:T(8,128)} custom-call(s32[2]{0:T(128)S(1)} %pad_add_fusion.1.at_ref, f32[128,1024]{1,0:T(8,128)S(1)} %fusion.1.scale_ref, bf16[2,128,1024]{2,1,0:T(8,128)(2,1)S(1)} %correlate.14.refs_0_, bf16[2,128,1024]{2,1,0:T(8,128)(2,1)S(1)} %collective-permute-done.6.refs_1_), custom_call_target="tpu_custom_call" | custom-call | flops 524288 | bytes 4194304 | tf_op jit(solution)/shard_map/scaled/pallas_call | solution.py:279
  120.1 1.0 scaled.6.refs_1_
  121.1 1.0 scaled.7.refs_1_
  122.2 7.4 %collective-permute-done.3.refs_0_ = bf16[2,128,1024]{2,1,0:T(8,128)(2,1)S(1)} collective-permute-done((bf16[2,128,1024]{2,1,0:T(8,128)(2,1)S(1)}, bf16[2,128,1024]{2,1,0:T(8,128)(2,1)S(1)}, u32[]{:S(2)}, u32[]{:S(2)}) %collective-permute-start.3) | collective-permute-done | bytes 524320 | tf_op jit(solution)/shard_map/ppermute | solution.py:321
  129.6 1.0 scaled.8.refs_3_
  130.6 7.0 %collective-permute-done.1.refs_1_ = bf16[2,128,1024]{2,1,0:T(8,128)(2,1)S(1)} collective-permute-done((bf16[2,128,1024]{2,1,0:T(8,128)(2,1)S(1)}, bf16[2,128,1024]{2,1,0:T(8,128)(2,1)S(1)}, u32[]{:S(2)}, u32[]{:S(2)}) %collective-permute-start.1) | collective-permute-done | bytes 524320 | tf_op jit(solution)/shard_map/ppermute | solution.py:321
  137.7 3.0 %collective-permute-done.refs_0_ = bf16[2,128,1024]{2,1,0:T(8,128)(2,1)S(1)} collective-permute-done((bf16[2,128,1024]{2,1,0:T(8,128)(2,1)S(1)}, bf16[2,128,1024]{2,1,0:T(8,128)(2,1)S(1)}, u32[]{:S(2)}, u32[]{:S(2)}) %collective-permute-start) | collective-permute-done | bytes 524320 | tf_op jit(solution)/shard_map/ppermute | solution.py:321
  140.7 2.3 %scaled.9 = f32[16,128,1024]{2,1,0:T(8,128)} custom-call(s32[3]{0:T(128)S(1)} %pad_add_fusion.at_ref, f32[128,1024]{1,0:T(8,128)S(1)} %fusion.1.scale_ref, bf16[2,128,1024]{2,1,0:T(8,128)(2,1)S(1)} %collective-permute-done.refs_0_, bf16[2,128,1024]{2,1,0:T(8,128)(2,1)S(1)} %collective-permute-done.1.refs_1_, ...), custom_call_target="tpu_custom_call", output_to_operand_aliasing={{}: (5, {})} | custom-call | flops 786432 | bytes 6291456 | tf_op jit(solution)/shard_map/scaled/pallas_call | solution.py:279
  (15 shorter events, 0.6 us)
Async XLA Ops:
  0.0 37.1 %copy-start.1 = (f32[2,16,256]{2,1,0:T(8,128)S(1)}, f32[2,16,256]{2,1,0:T(8,128)}, u32[]{:S(2)}) copy-start(f32[2,16,256]{2,1,0:T(8,128)} %constant.40.clone.twiddle_hbm) | copy-start | bytes 98308
  0.0 37.1 %copy-start = (f32[16,4096]{1,0:T(8,128)S(1)}, f32[16,4096]{1,0:T(8,128)}, u32[]{:S(2)}) copy-start(f32[16,4096]{1,0:T(8,128)} %rows_ref.1) | copy-start | bytes 786436
  0.0 37.1 %all-to-all-start = ((bf16[16,8,2,4096]{3,2,1,0:T(2,128)(2,1)}), bf16[16,8,2,4096]{3,2,1,0:T(2,128)(2,1)S(1)}, u32[]{:S(2)}, u32[]{:S(2)}) async-start(bf16[16,8,2,4096]{3,2,1,0:T(2,128)(2,1)} %bitcast.22), calls=%async_computation | async-start | bytes 4194304 | tf_op jit(solution)/shard_map/all_to_all | solution.py:309
  9.8 0.8 copy-start.2
  90.7 15.2 %collective-permute-start.6 = (bf16[2,128,1024]{2,1,0:T(8,128)(2,1)S(1)}, bf16[2,128,1024]{2,1,0:T(8,128)(2,1)S(1)}, u32[]{:S(2)}, u32[]{:S(2)}) collective-permute-start(bf16[2,128,1024]{2,1,0:T(8,128)(2,1)S(1)} %correlate.15), channel_id=1, source_target_pairs={{0,6},{1,7},{2,4},{3,5},{4,2},{5,3},{6,0},{7,1},{8,14},{9,15},{10,... | collective-permute-start | bytes 1572872 | tf_op jit(solution)/shard_map/ppermute | solution.py:321
  91.7 22.6 %collective-permute-start.5 = (bf16[2,128,1024]{2,1,0:T(8,128)(2,1)S(1)}, bf16[2,128,1024]{2,1,0:T(8,128)(2,1)S(1)}, u32[]{:S(2)}, u32[]{:S(2)}) collective-permute-start(bf16[2,128,1024]{2,1,0:T(8,128)(2,1)S(1)} %correlate.13), channel_id=1, source_target_pairs={{0,4},{1,5},{2,6},{3,7},{4,0},{5,1},{6,2},{7,3},{8,12},{9,13},{10,... | collective-permute-start | bytes 1572872 | tf_op jit(solution)/shard_map/ppermute | solution.py:321
  93.8 27.3 %collective-permute-start.4 = (bf16[2,128,1024]{2,1,0:T(8,128)(2,1)S(1)}, bf16[2,128,1024]{2,1,0:T(8,128)(2,1)S(1)}, u32[]{:S(2)}, u32[]{:S(2)}) collective-permute-start(bf16[2,128,1024]{2,1,0:T(8,128)(2,1)S(1)} %correlate.12), channel_id=1, source_target_pairs={{0,2},{1,3},{2,0},{3,1},{4,6},{5,7},{6,4},{7,5},{8,10},{9,11},{10,... | collective-permute-start | bytes 1572872 | tf_op jit(solution)/shard_map/ppermute | solution.py:321
  97.5 32.0 %collective-permute-start.3 = (bf16[2,128,1024]{2,1,0:T(8,128)(2,1)S(1)}, bf16[2,128,1024]{2,1,0:T(8,128)(2,1)S(1)}, u32[]{:S(2)}, u32[]{:S(2)}) collective-permute-start(bf16[2,128,1024]{2,1,0:T(8,128)(2,1)S(1)} %correlate.11), channel_id=1, source_target_pairs={{0,1},{1,0},{2,3},{3,2},{4,5},{5,4},{6,7},{7,6},{8,9},{9,8},{10,11... | collective-permute-start | bytes 1572872 | tf_op jit(solution)/shard_map/ppermute | solution.py:321
  98.6 32.0 %collective-permute-start.2 = (bf16[2,128,1024]{2,1,0:T(8,128)(2,1)S(1)}, bf16[2,128,1024]{2,1,0:T(8,128)(2,1)S(1)}, u32[]{:S(2)}, u32[]{:S(2)}) collective-permute-start(bf16[2,128,1024]{2,1,0:T(8,128)(2,1)S(1)} %correlate.10), channel_id=1, source_target_pairs={{0,7},{1,6},{2,5},{3,4},{4,3},{5,2},{6,1},{7,0},{8,15},{9,14},{10,... | collective-permute-start | bytes 1572872 | tf_op jit(solution)/shard_map/ppermute | solution.py:321
  105.9 31.8 %collective-permute-start.1 = (bf16[2,128,1024]{2,1,0:T(8,128)(2,1)S(1)}, bf16[2,128,1024]{2,1,0:T(8,128)(2,1)S(1)}, u32[]{:S(2)}, u32[]{:S(2)}) collective-permute-start(bf16[2,128,1024]{2,1,0:T(8,128)(2,1)S(1)} %correlate.9), channel_id=1, source_target_pairs={{0,5},{1,4},{2,7},{3,6},{4,1},{5,0},{6,3},{7,2},{8,13},{9,12},{10,... | collective-permute-start | bytes 1572872 | tf_op jit(solution)/shard_map/ppermute | solution.py:321
  114.3 26.4 %collective-permute-start = (bf16[2,128,1024]{2,1,0:T(8,128)(2,1)S(1)}, bf16[2,128,1024]{2,1,0:T(8,128)(2,1)S(1)}, u32[]{:S(2)}, u32[]{:S(2)}) collective-permute-start(bf16[2,128,1024]{2,1,0:T(8,128)(2,1)S(1)} %correlate.8), channel_id=1, source_target_pairs={{0,3},{1,2},{2,1},{3,0},{4,7},{5,6},{6,5},{7,4},{8,11},{9,10},{10,... | collective-permute-start | bytes 1572872 | tf_op jit(solution)/shard_map/ppermute | solution.py:321

commit v5 on v4

--- a/solution.py
+++ b/solution.py
@@ -12,8 +12,8 @@
 AVG = 16
 LANES = 128
 BLOCK = 256
-TOGETHER = ((6,), (4,), (2,), (1,), (3,), (5,), (7,), (0,))
-ARRIVING = ((0, 6), (4,), (2,), (1,), (3, 5, 7))
+TOGETHER = ((6,), (4,), (2,), (1,), (3,), (7,), (5,), (0,))
+ARRIVING = ((0, 6), (4,), (2,), (1,), (3, 7, 5))
 INNER = 256
 F32 = jnp.float32
 BF16 = jnp.bfloat16
@@ -74,8 +74,8 @@
 
 
 def channelize_kernel(
-    x_ref, rows_ref, keep_hbm, twiddle_hbm, second_hbm, out_hbm,
-    window, stage_even, stage_odd, turned, out, taps_ref, keep_ref, twiddle_ref, second_ref, table_sems, out_sems,
+    x_ref, rows_ref, keep_hbm, twiddle_hbm, second_hbm, out,
+    window, stage_even, stage_odd, turned, taps_ref, keep_ref, twiddle_ref, second_ref, table_sems,
 ):
     sources, signals, per_source, channels = x_ref.shape
     taps = taps_ref.shape[0]
@@ -161,10 +161,6 @@
     step_groups = 32
     step_rows = step_groups // 2 * signals
 
-    def out_copy(step):
-        rows = pl.ds(pl.multiple_of(step * step_rows, step_rows), step_rows)
-        return pltpu.make_async_copy(out.at[rows, :], out_hbm.at[rows, :], out_sems.at[step])
-
     def last(step, carry):
         rows = pl.ds(pl.multiple_of(step * step_rows, step_rows), step_rows)
         for c in range(columns // LANES):
@@ -177,13 +173,9 @@
                     axis=0,
                 )
                 out[rows, pl.ds(pair * columns + c * LANES, LANES)] = value.astype(BF16)
-        out_copy(step).start()
         return carry
 
-    steps = groups // step_groups
-    lax.fori_loop(0, steps, last, 0)
-    for step in range(steps):
-        out_copy(step).wait()
+    lax.fori_loop(0, groups // step_groups, last, 0)
 
 
 def channelize(x, taps, keep, twiddle, second):
@@ -199,19 +191,17 @@
         channelize_kernel,
         out_shape=jax.ShapeDtypeStruct(shape, BF16),
         in_specs=[whole] * 2 + [hbm] * 3,
-        out_specs=hbm,
+        out_specs=whole,
         scratch_shapes=[
             pltpu.VMEM((signals * frames * (lane_blocks + 1), LANES), F32),
             pltpu.VMEM((columns, 4 * INNER), BF16),
             pltpu.VMEM((columns, 4 * INNER), BF16),
             pltpu.VMEM((columns // LANES, groups * (signals + 1), LANES), F32),
-            pltpu.VMEM(shape, BF16),
             pltpu.VMEM((taps.shape[0], lane_blocks, LANES), F32),
             pltpu.VMEM(keep.shape, F32),
             pltpu.VMEM(twiddle.shape, F32),
             pltpu.VMEM(second.shape, BF16),
             pltpu.SemaphoreType.DMA((3,)),
-            pltpu.SemaphoreType.DMA((groups // 32,)),
         ],
         compiler_params=pltpu.CompilerParams(vmem_limit_bytes=28 * 1024 * 1024),
         name="channelize",

time: 143 us -> 143 us (level)
  waiting for transfers between devices: 54.6 us -> 52.9 us
    ppermute x7, waiting for transfers between devices: 31 us -> 29.3 us  [body(): sent[distance] = lax.ppermute(tile, 'stn', route) if distance else tile]
  transfers between devices with their start and end apart: 8 -> 8, of which waited for: 6 -> 4; matrix products, arithmetic and copies ran while one was open for 3% -> 3% of each run, Pallas kernels for 8% -> 8%
where the time goes in v5:
time: 143 us; the launch traced here: 142 us
  waiting for transfers between devices  52.9 us (37%)
  blocking collectives  40.5 us (28%)
  Pallas kernels  25.9 us (18%)
  starting transfers between devices  17.4 us (12%)
  other arithmetic  2.06 us (1%)
  matrix products  1.73 us (1%)
    all_to_all x1, blocking collectives, body(): lax.all_to_all(kept, ('stn', 'freq'), split_axis=0, concat_axis=0, tiled=...  40.5 us
    ppermute x7, waiting for transfers between devices, body(): sent[distance] = lax.ppermute(tile, 'stn', route) if distance else tile  29.3 us
    all_to_all x1, waiting for transfers between devices, body(): lax.all_to_all(voltages.reshape(n_freq, own, spec_dev, channels), 'freq',...  23.6 us
    pallas_call x1, Pallas kernels, channelize(): pl.pallas_call(channelize_kernel, out_shape=jax.ShapeDtypeStruct(shape, B...  12 us
    ppermute x7, starting transfers between devices, body(): sent[distance] = lax.ppermute(tile, 'stn', route) if distance else tile  8.8 us
    all_to_all x1, starting transfers between devices, body(): lax.all_to_all(voltages.reshape(n_freq, own, spec_dev, channels), 'freq',...  8.58 us
    pallas_call x5, Pallas kernels, scaled(): pl.pallas_call(functools.partial(scale_kernel, count), out_shape=jax.Shap...  7.33 us
    pallas_call x8, Pallas kernels, correlate(): pl.pallas_call(correlate_kernel, out_shape=(jax.ShapeDtypeStruct((2, rows...  6.57 us
  transfers between devices with their start and end apart: 8, of which 4 were waited for; matrix products, arithmetic and copies ran while one was open for 3% of the time, Pallas kernels for 8%

profile of v5, /device:TPU:1, one launch (start us, length us, event | category | flops | bytes accessed | tf_op | source)
XLA Modules:
  0.0 142.0 jit_solution(17292789885441610269)
XLA Ops:
  0.0 8.6 %all-to-all-start = ((bf16[16,8,2,4096]{3,2,1,0:T(2,128)(2,1)}), bf16[16,8,2,4096]{3,2,1,0:T(2,128)(2,1)S(1)}, u32[]{:S(2)}, u32[]{:S(2)}) async-start(bf16[16,8,2,4096]{3,2,1,0:T(2,128)(2,1)} %bitcast.22), calls=%async_computation | async-start | bytes 4194304 | tf_op jit(solution)/shard_map/all_to_all | solution.py:299
  8.6 0.8 convert_element_type.16
  9.4 0.1 copy.10
  9.6 0.2 broadcast_in_dim.3
  9.8 0.8 copy-done.2
  10.6 1.1 pad_maximum_fusion.second_hbm
  11.7 1.7 %fusion.1.scale_ref = f32[128,1024]{1,0:T(8,128)S(1)} fusion(f32[1024,32]{1,0:T(8,128)} %bitcast.24, s32[]{:T(128)S(6)} %select_n.7), kind=kOutput, calls=%fused_computation.2 | convolution fusion | flops 50724864 | bytes 1114116 | tf_op jit(solution)/shard_map/dot_general | solution.py:302
  13.4 23.6 %all-to-all-done.x_ref = bf16[16,8,2,4096]{3,2,1,0:T(2,128)(2,1)S(1)} async-done(((bf16[16,8,2,4096]{3,2,1,0:T(2,128)(2,1)}), bf16[16,8,2,4096]{3,2,1,0:T(2,128)(2,1)S(1)}, u32[]{:S(2)}, u32[]{:S(2)}) %all-to-all-start) | async-done | bytes 2097184 | tf_op jit(solution)/shard_map/all_to_all | solution.py:299
  37.1 12.0 %channelize.1 = bf16[1024,1024]{1,0:T(8,128)(2,1)S(1)} custom-call(bf16[16,8,2,4096]{3,2,1,0:T(2,128)(2,1)S(1)} %all-to-all-done.x_ref, f32[16,4096]{1,0:T(8,128)S(1)} %copy-done, f32[8,128]{1,0:T(8,128)S(1)} %tile.10.keep_hbm, f32[2,16,256]{2,1,0:T(8,128)S(1)} %copy-done.1, bf16[512,512]{1,0:T(8,128)(2,1)S(1)} %pad_maximum_fusion.second_hbm), custom_call_target="tpu_custom_call" | custom-call | tf_op jit(solution)/shard_map/channelize/pallas_call | solution.py:190
  49.1 40.5 %all_to_all.16 = bf16[128,8,1024]{2,1,0:T(8,128)(2,1)S(1)} all-to-all(bf16[128,8,1024]{2,1,0:T(8,128)(2,1)S(1)} %bitcast.21), channel_id=1, replica_groups=mesh['freq'=16,'stn'=8] {'stn','freq'}, dimensions={0} | all-to-all | bytes 4194304 | tf_op jit(solution)/shard_map/all_to_all | solution.py:306
  89.6 0.8 correlate.15
  90.4 0.2 collective-permute-start.6
  90.6 0.8 correlate.13
  91.4 1.3 collective-permute-start.5
  92.8 0.8 correlate.12
  93.6 2.9 %collective-permute-start.4 = (bf16[2,128,1024]{2,1,0:T(8,128)(2,1)S(1)}, bf16[2,128,1024]{2,1,0:T(8,128)(2,1)S(1)}, u32[]{:S(2)}, u32[]{:S(2)}) collective-permute-start(bf16[2,128,1024]{2,1,0:T(8,128)(2,1)S(1)} %correlate.12), channel_id=1, source_target_pairs={{0,2},{1,3},{2,0},{3,1},{4,6},{5,7},{6,4},{7,5},{8,10},{9,11},{10,... | collective-permute-start | bytes 1572872 | tf_op jit(solution)/shard_map/ppermute | solution.py:311
  96.5 0.8 correlate.11
  97.3 0.3 collective-permute-start.3
  97.6 0.8 correlate.10
  98.4 1.3 collective-permute-start.2
  99.7 0.8 correlate.9
  100.5 0.8 correlate.8
  101.3 4.3 %collective-permute-done.6.refs_1_ = bf16[2,128,1024]{2,1,0:T(8,128)(2,1)S(1)} collective-permute-done((bf16[2,128,1024]{2,1,0:T(8,128)(2,1)S(1)}, bf16[2,128,1024]{2,1,0:T(8,128)(2,1)S(1)}, u32[]{:S(2)}, u32[]{:S(2)}) %collective-permute-start.6) | collective-permute-done | bytes 524320 | tf_op jit(solution)/shard_map/ppermute | solution.py:311
  105.7 8.3 %collective-permute-done.5.refs_0_ = bf16[2,128,1024]{2,1,0:T(8,128)(2,1)S(1)} collective-permute-done((bf16[2,128,1024]{2,1,0:T(8,128)(2,1)S(1)}, bf16[2,128,1024]{2,1,0:T(8,128)(2,1)S(1)}, u32[]{:S(2)}, u32[]{:S(2)}) %collective-permute-start.5) | collective-permute-done | bytes 524320 | tf_op jit(solution)/shard_map/ppermute | solution.py:311
  114.0 2.9 %collective-permute-start = (bf16[2,128,1024]{2,1,0:T(8,128)(2,1)S(1)}, bf16[2,128,1024]{2,1,0:T(8,128)(2,1)S(1)}, u32[]{:S(2)}, u32[]{:S(2)}) collective-permute-start(bf16[2,128,1024]{2,1,0:T(8,128)(2,1)S(1)} %correlate.8), channel_id=1, source_target_pairs={{0,3},{1,2},{2,1},{3,0},{4,7},{5,6},{6,5},{7,4},{8,11},{9,10},{10,... | collective-permute-start | bytes 1572872 | tf_op jit(solution)/shard_map/ppermute | solution.py:311
  117.0 0.8 correlate.14.refs_0_
  117.8 2.0 %scaled.5.refs_1_ = f32[16,128,1024]{2,1,0:T(8,128)} custom-call(s32[2]{0:T(128)S(1)} %pad_add_fusion.1.at_ref, f32[128,1024]{1,0:T(8,128)S(1)} %fusion.1.scale_ref, bf16[2,128,1024]{2,1,0:T(8,128)(2,1)S(1)} %correlate.14.refs_0_, bf16[2,128,1024]{2,1,0:T(8,128)(2,1)S(1)} %collective-permute-done.6.refs_1_), custom_call_target="tpu_custom_call" | custom-call | flops 524288 | bytes 4194304 | tf_op jit(solution)/shard_map/scaled/pallas_call | solution.py:269
  119.8 1.0 scaled.6.refs_1_
  120.9 1.0 scaled.7.refs_1_
  121.9 16.6 %collective-permute-done.3.refs_0_ = bf16[2,128,1024]{2,1,0:T(8,128)(2,1)S(1)} collective-permute-done((bf16[2,128,1024]{2,1,0:T(8,128)(2,1)S(1)}, bf16[2,128,1024]{2,1,0:T(8,128)(2,1)S(1)}, u32[]{:S(2)}, u32[]{:S(2)}) %collective-permute-start.3) | collective-permute-done | bytes 524320 | tf_op jit(solution)/shard_map/ppermute | solution.py:311
  138.5 1.0 scaled.8.refs_3_
  139.5 2.3 %scaled.9 = f32[16,128,1024]{2,1,0:T(8,128)} custom-call(s32[3]{0:T(128)S(1)} %pad_add_fusion.at_ref, f32[128,1024]{1,0:T(8,128)S(1)} %fusion.1.scale_ref, bf16[2,128,1024]{2,1,0:T(8,128)(2,1)S(1)} %collective-permute-done.refs_0_, bf16[2,128,1024]{2,1,0:T(8,128)(2,1)S(1)} %collective-permute-done.1.refs_1_, ...), custom_call_target="tpu_custom_call", output_to_operand_aliasing={{}: (5, {})} | custom-call | flops 786432 | bytes 6291456 | tf_op jit(solution)/shard_map/scaled/pallas_call | solution.py:269
  (15 shorter events, 0.3 us)
Async XLA Ops:
  0.0 37.1 %copy-start.1 = (f32[2,16,256]{2,1,0:T(8,128)S(1)}, f32[2,16,256]{2,1,0:T(8,128)}, u32[]{:S(2)}) copy-start(f32[2,16,256]{2,1,0:T(8,128)} %constant.40.clone.twiddle_hbm) | copy-start | bytes 98308
  0.0 37.1 %copy-start = (f32[16,4096]{1,0:T(8,128)S(1)}, f32[16,4096]{1,0:T(8,128)}, u32[]{:S(2)}) copy-start(f32[16,4096]{1,0:T(8,128)} %rows_ref.1) | copy-start | bytes 786436
  0.0 37.1 %all-to-all-start = ((bf16[16,8,2,4096]{3,2,1,0:T(2,128)(2,1)}), bf16[16,8,2,4096]{3,2,1,0:T(2,128)(2,1)S(1)}, u32[]{:S(2)}, u32[]{:S(2)}) async-start(bf16[16,8,2,4096]{3,2,1,0:T(2,128)(2,1)} %bitcast.22), calls=%async_computation | async-start | bytes 4194304 | tf_op jit(solution)/shard_map/all_to_all | solution.py:299
  9.8 0.8 copy-start.2
  90.4 15.2 %collective-permute-start.6 = (bf16[2,128,1024]{2,1,0:T(8,128)(2,1)S(1)}, bf16[2,128,1024]{2,1,0:T(8,128)(2,1)S(1)}, u32[]{:S(2)}, u32[]{:S(2)}) collective-permute-start(bf16[2,128,1024]{2,1,0:T(8,128)(2,1)S(1)} %correlate.15), channel_id=1, source_target_pairs={{0,6},{1,7},{2,4},{3,5},{4,2},{5,3},{6,0},{7,1},{8,14},{9,15},{10,... | collective-permute-start | bytes 1572872 | tf_op jit(solution)/shard_map/ppermute | solution.py:311
  91.4 22.6 %collective-permute-start.5 = (bf16[2,128,1024]{2,1,0:T(8,128)(2,1)S(1)}, bf16[2,128,1024]{2,1,0:T(8,128)(2,1)S(1)}, u32[]{:S(2)}, u32[]{:S(2)}) collective-permute-start(bf16[2,128,1024]{2,1,0:T(8,128)(2,1)S(1)} %correlate.13), channel_id=1, source_target_pairs={{0,4},{1,5},{2,6},{3,7},{4,0},{5,1},{6,2},{7,3},{8,12},{9,13},{10,... | collective-permute-start | bytes 1572872 | tf_op jit(solution)/shard_map/ppermute | solution.py:311
  93.6 27.3 %collective-permute-start.4 = (bf16[2,128,1024]{2,1,0:T(8,128)(2,1)S(1)}, bf16[2,128,1024]{2,1,0:T(8,128)(2,1)S(1)}, u32[]{:S(2)}, u32[]{:S(2)}) collective-permute-start(bf16[2,128,1024]{2,1,0:T(8,128)(2,1)S(1)} %correlate.12), channel_id=1, source_target_pairs={{0,2},{1,3},{2,0},{3,1},{4,6},{5,7},{6,4},{7,5},{8,10},{9,11},{10,... | collective-permute-start | bytes 1572872 | tf_op jit(solution)/shard_map/ppermute | solution.py:311
  97.3 41.2 %collective-permute-start.3 = (bf16[2,128,1024]{2,1,0:T(8,128)(2,1)S(1)}, bf16[2,128,1024]{2,1,0:T(8,128)(2,1)S(1)}, u32[]{:S(2)}, u32[]{:S(2)}) collective-permute-start(bf16[2,128,1024]{2,1,0:T(8,128)(2,1)S(1)} %correlate.11), channel_id=1, source_target_pairs={{0,1},{1,0},{2,3},{3,2},{4,5},{5,4},{6,7},{7,6},{8,9},{9,8},{10,11... | collective-permute-start | bytes 1572872 | tf_op jit(solution)/shard_map/ppermute | solution.py:311
  98.4 41.1 %collective-permute-start.2 = (bf16[2,128,1024]{2,1,0:T(8,128)(2,1)S(1)}, bf16[2,128,1024]{2,1,0:T(8,128)(2,1)S(1)}, u32[]{:S(2)}, u32[]{:S(2)}) collective-permute-start(bf16[2,128,1024]{2,1,0:T(8,128)(2,1)S(1)} %correlate.10), channel_id=1, source_target_pairs={{0,5},{1,4},{2,7},{3,6},{4,1},{5,0},{6,3},{7,2},{8,13},{9,12},{10,... | collective-permute-start | bytes 1572872 | tf_op jit(solution)/shard_map/ppermute | solution.py:311
  105.7 33.9 %collective-permute-start.1 = (bf16[2,128,1024]{2,1,0:T(8,128)(2,1)S(1)}, bf16[2,128,1024]{2,1,0:T(8,128)(2,1)S(1)}, u32[]{:S(2)}, u32[]{:S(2)}) collective-permute-start(bf16[2,128,1024]{2,1,0:T(8,128)(2,1)S(1)} %correlate.9), channel_id=1, source_target_pairs={{0,7},{1,6},{2,5},{3,4},{4,3},{5,2},{6,1},{7,0},{8,15},{9,14},{10,... | collective-permute-start | bytes 1572872 | tf_op jit(solution)/shard_map/ppermute | solution.py:311
  114.0 25.5 %collective-permute-start = (bf16[2,128,1024]{2,1,0:T(8,128)(2,1)S(1)}, bf16[2,128,1024]{2,1,0:T(8,128)(2,1)S(1)}, u32[]{:S(2)}, u32[]{:S(2)}) collective-permute-start(bf16[2,128,1024]{2,1,0:T(8,128)(2,1)S(1)} %correlate.8), channel_id=1, source_target_pairs={{0,3},{1,2},{2,1},{3,0},{4,7},{5,6},{6,5},{7,4},{8,11},{9,10},{10,... | collective-permute-start | bytes 1572872 | tf_op jit(solution)/shard_map/ppermute | solution.py:311

commit v6 on v5

--- a/solution.py
+++ b/solution.py
@@ -74,8 +74,8 @@
 
 
 def channelize_kernel(
-    x_ref, rows_ref, keep_hbm, twiddle_hbm, second_hbm, out,
-    window, stage_even, stage_odd, turned, taps_ref, keep_ref, twiddle_ref, second_ref, table_sems,
+    x_ref, rows_ref, keep_ref, twiddle_ref, second_ref, out,
+    window, stage_even, stage_odd, turned, taps_ref,
 ):
     sources, signals, per_source, channels = x_ref.shape
     taps = taps_ref.shape[0]
@@ -85,14 +85,6 @@
     lane_blocks = channels // LANES
     chunk = 8 * LANES
 
-    tables = [
-        pltpu.make_async_copy(source, target, table_sems.at[n])
-        for n, (source, target) in enumerate(
-            ((keep_hbm, keep_ref), (twiddle_hbm, twiddle_ref), (second_hbm, second_ref))
-        )
-    ]
-    for copy in tables:
-        copy.start()
     for t in range(taps):
         for c in range(channels // chunk):
             taps_ref[t, c * 8 : (c + 1) * 8, :] = rows_ref[t : t + 1, c * chunk : (c + 1) * chunk].reshape(8, LANES)
@@ -117,8 +109,6 @@
         return carry
 
     lax.fori_loop(0, signals * (channels // chunk), fir, 0)
-    for copy in tables:
-        copy.wait()
 
     columns = AVG * frames
     stages = (stage_even, stage_odd)
@@ -185,12 +175,11 @@
     columns = AVG * frames
     lane_blocks = channels // LANES
     whole = pl.BlockSpec(memory_space=pltpu.VMEM)
-    hbm = pl.BlockSpec(memory_space=pltpu.HBM)
     shape = (groups // 2 * signals, 2 * columns)
     return pl.pallas_call(
         channelize_kernel,
         out_shape=jax.ShapeDtypeStruct(shape, BF16),
-        in_specs=[whole] * 2 + [hbm] * 3,
+        in_specs=[whole] * 5,
         out_specs=whole,
         scratch_shapes=[
             pltpu.VMEM((signals * frames * (lane_blocks + 1), LANES), F32),
@@ -198,10 +187,6 @@
             pltpu.VMEM((columns, 4 * INNER), BF16),
             pltpu.VMEM((columns // LANES, groups * (signals + 1), LANES), F32),
             pltpu.VMEM((taps.shape[0], lane_blocks, LANES), F32),
-            pltpu.VMEM(keep.shape, F32),
-            pltpu.VMEM(twiddle.shape, F32),
-            pltpu.VMEM(second.shape, BF16),
-            pltpu.SemaphoreType.DMA((3,)),
         ],
         compiler_params=pltpu.CompilerParams(vmem_limit_bytes=28 * 1024 * 1024),
         name="channelize",

time: 143 us -> 143 us (level)
  no operation moved by 1% of the time
where the time goes in v6:
time: 143 us
  waiting for transfers between devices  52.9 us (37%)
  blocking collectives  40.5 us (28%)
  Pallas kernels  26.5 us (19%)
  starting transfers between devices  17.4 us (12%)
  other arithmetic  2.06 us (1%)
  matrix products  1.73 us (1%)
    all_to_all x1, blocking collectives, body(): lax.all_to_all(kept, ('stn', 'freq'), split_axis=0, concat_axis=0, tiled=...  40.5 us
    ppermute x7, waiting for transfers between devices, body(): sent[distance] = lax.ppermute(tile, 'stn', route) if distance else tile  29.3 us
    all_to_all x1, waiting for transfers between devices, body(): lax.all_to_all(voltages.reshape(n_freq, own, spec_dev, channels), 'freq',...  23.6 us
    pallas_call x1, Pallas kernels, channelize(): pl.pallas_call(channelize_kernel, out_shape=jax.ShapeDtypeStruct(shape, B...  12.6 us
    ppermute x7, starting transfers between devices, body(): sent[distance] = lax.ppermute(tile, 'stn', route) if distance else tile  8.8 us
    all_to_all x1, starting transfers between devices, body(): lax.all_to_all(voltages.reshape(n_freq, own, spec_dev, channels), 'freq',...  8.58 us
    pallas_call x5, Pallas kernels, scaled(): pl.pallas_call(functools.partial(scale_kernel, count), out_shape=jax.Shap...  7.33 us
    pallas_call x8, Pallas kernels, correlate(): pl.pallas_call(correlate_kernel, out_shape=(jax.ShapeDtypeStruct((2, rows...  6.57 us
  transfers between devices with their start and end apart: 8, of which 4 were waited for; matrix products, arithmetic and copies ran while one was open for 3% of the time, Pallas kernels for 8%

profile of v6, /device:TPU:1, one launch (start us, length us, event | category | flops | bytes accessed | tf_op | source)
XLA Modules:
  0.0 142.6 jit_solution(17522609006085715736)
XLA Ops:
  0.0 8.6 %all-to-all-start = ((bf16[16,8,2,4096]{3,2,1,0:T(2,128)(2,1)}), bf16[16,8,2,4096]{3,2,1,0:T(2,128)(2,1)S(1)}, u32[]{:S(2)}, u32[]{:S(2)}) async-start(bf16[16,8,2,4096]{3,2,1,0:T(2,128)(2,1)} %bitcast.22), calls=%async_computation | async-start | bytes 4194304 | tf_op jit(solution)/shard_map/all_to_all | solution.py:284
  8.6 0.8 convert_element_type.16
  9.4 0.1 copy.10
  9.6 0.2 broadcast_in_dim.3
  9.8 0.8 copy-done.2
  10.6 1.1 pad_maximum_fusion.second_ref
  11.7 1.7 %fusion.1.scale_ref = f32[128,1024]{1,0:T(8,128)S(1)} fusion(f32[1024,32]{1,0:T(8,128)} %bitcast.24, s32[]{:T(128)S(6)} %select_n.7), kind=kOutput, calls=%fused_computation.2 | convolution fusion | flops 50724864 | bytes 1114116 | tf_op jit(solution)/shard_map/dot_general | solution.py:287
  13.4 23.6 %all-to-all-done.x_ref = bf16[16,8,2,4096]{3,2,1,0:T(2,128)(2,1)S(1)} async-done(((bf16[16,8,2,4096]{3,2,1,0:T(2,128)(2,1)}), bf16[16,8,2,4096]{3,2,1,0:T(2,128)(2,1)S(1)}, u32[]{:S(2)}, u32[]{:S(2)}) %all-to-all-start) | async-done | bytes 2097184 | tf_op jit(solution)/shard_map/all_to_all | solution.py:284
  37.1 12.6 %channelize.1 = bf16[1024,1024]{1,0:T(8,128)(2,1)S(1)} custom-call(bf16[16,8,2,4096]{3,2,1,0:T(2,128)(2,1)S(1)} %all-to-all-done.x_ref, f32[16,4096]{1,0:T(8,128)S(1)} %copy-done, f32[8,128]{1,0:T(8,128)S(1)} %tile.10.keep_ref, f32[2,16,256]{2,1,0:T(8,128)S(1)} %copy-done.1, bf16[512,512]{1,0:T(8,128)(2,1)S(1)} %pad_maximum_fusion.second_ref), custom_call_target="tpu_custom_call" | custom-call | tf_op jit(solution)/shard_map/channelize/pallas_call | solution.py:179
  49.6 40.5 %all_to_all.16 = bf16[128,8,1024]{2,1,0:T(8,128)(2,1)S(1)} all-to-all(bf16[128,8,1024]{2,1,0:T(8,128)(2,1)S(1)} %bitcast.21), channel_id=1, replica_groups=mesh['freq'=16,'stn'=8] {'stn','freq'}, dimensions={0} | all-to-all | bytes 4194304 | tf_op jit(solution)/shard_map/all_to_all | solution.py:291
  90.1 0.8 correlate.15
  91.0 0.2 collective-permute-start.6
  91.1 0.8 correlate.13
  92.0 1.3 collective-permute-start.5
  93.3 0.8 correlate.12
  94.1 2.9 %collective-permute-start.4 = (bf16[2,128,1024]{2,1,0:T(8,128)(2,1)S(1)}, bf16[2,128,1024]{2,1,0:T(8,128)(2,1)S(1)}, u32[]{:S(2)}, u32[]{:S(2)}) collective-permute-start(bf16[2,128,1024]{2,1,0:T(8,128)(2,1)S(1)} %correlate.12), channel_id=1, source_target_pairs={{0,2},{1,3},{2,0},{3,1},{4,6},{5,7},{6,4},{7,5},{8,10},{9,11},{10,... | collective-permute-start | bytes 1572872 | tf_op jit(solution)/shard_map/ppermute | solution.py:296
  97.0 0.8 correlate.11
  97.8 0.3 collective-permute-start.3
  98.1 0.8 correlate.10
  98.9 1.3 collective-permute-start.2
  100.2 0.8 correlate.9
  101.0 0.8 correlate.8
  101.9 4.3 %collective-permute-done.6.refs_1_ = bf16[2,128,1024]{2,1,0:T(8,128)(2,1)S(1)} collective-permute-done((bf16[2,128,1024]{2,1,0:T(8,128)(2,1)S(1)}, bf16[2,128,1024]{2,1,0:T(8,128)(2,1)S(1)}, u32[]{:S(2)}, u32[]{:S(2)}) %collective-permute-start.6) | collective-permute-done | bytes 524320 | tf_op jit(solution)/shard_map/ppermute | solution.py:296
  106.2 8.3 %collective-permute-done.5.refs_0_ = bf16[2,128,1024]{2,1,0:T(8,128)(2,1)S(1)} collective-permute-done((bf16[2,128,1024]{2,1,0:T(8,128)(2,1)S(1)}, bf16[2,128,1024]{2,1,0:T(8,128)(2,1)S(1)}, u32[]{:S(2)}, u32[]{:S(2)}) %collective-permute-start.5) | collective-permute-done | bytes 524320 | tf_op jit(solution)/shard_map/ppermute | solution.py:296
  114.5 2.9 %collective-permute-start = (bf16[2,128,1024]{2,1,0:T(8,128)(2,1)S(1)}, bf16[2,128,1024]{2,1,0:T(8,128)(2,1)S(1)}, u32[]{:S(2)}, u32[]{:S(2)}) collective-permute-start(bf16[2,128,1024]{2,1,0:T(8,128)(2,1)S(1)} %correlate.8), channel_id=1, source_target_pairs={{0,3},{1,2},{2,1},{3,0},{4,7},{5,6},{6,5},{7,4},{8,11},{9,10},{10,... | collective-permute-start | bytes 1572872 | tf_op jit(solution)/shard_map/ppermute | solution.py:296
  117.5 0.8 correlate.14.refs_0_
  118.3 2.0 %scaled.5.refs_1_ = f32[16,128,1024]{2,1,0:T(8,128)} custom-call(s32[2]{0:T(128)S(1)} %pad_add_fusion.1.at_ref, f32[128,1024]{1,0:T(8,128)S(1)} %fusion.1.scale_ref, bf16[2,128,1024]{2,1,0:T(8,128)(2,1)S(1)} %correlate.14.refs_0_, bf16[2,128,1024]{2,1,0:T(8,128)(2,1)S(1)} %collective-permute-done.6.refs_1_), custom_call_target="tpu_custom_call" | custom-call | flops 524288 | bytes 4194304 | tf_op jit(solution)/shard_map/scaled/pallas_call | solution.py:254
  120.4 1.0 scaled.6.refs_1_
  121.4 1.0 scaled.7.refs_1_
  122.4 16.6 %collective-permute-done.3.refs_0_ = bf16[2,128,1024]{2,1,0:T(8,128)(2,1)S(1)} collective-permute-done((bf16[2,128,1024]{2,1,0:T(8,128)(2,1)S(1)}, bf16[2,128,1024]{2,1,0:T(8,128)(2,1)S(1)}, u32[]{:S(2)}, u32[]{:S(2)}) %collective-permute-start.3) | collective-permute-done | bytes 524320 | tf_op jit(solution)/shard_map/ppermute | solution.py:296
  139.0 1.0 scaled.8.refs_3_
  140.1 2.3 %scaled.9 = f32[16,128,1024]{2,1,0:T(8,128)} custom-call(s32[3]{0:T(128)S(1)} %pad_add_fusion.at_ref, f32[128,1024]{1,0:T(8,128)S(1)} %fusion.1.scale_ref, bf16[2,128,1024]{2,1,0:T(8,128)(2,1)S(1)} %collective-permute-done.refs_0_, bf16[2,128,1024]{2,1,0:T(8,128)(2,1)S(1)} %collective-permute-done.1.refs_1_, ...), custom_call_target="tpu_custom_call", output_to_operand_aliasing={{}: (5, {})} | custom-call | flops 786432 | bytes 6291456 | tf_op jit(solution)/shard_map/scaled/pallas_call | solution.py:254
  (15 shorter events, 0.3 us)
Async XLA Ops:
  0.0 37.1 %copy-start.1 = (f32[2,16,256]{2,1,0:T(8,128)S(1)}, f32[2,16,256]{2,1,0:T(8,128)}, u32[]{:S(2)}) copy-start(f32[2,16,256]{2,1,0:T(8,128)} %constant.40.clone.twiddle_ref) | copy-start | bytes 98308
  0.0 37.1 %copy-start = (f32[16,4096]{1,0:T(8,128)S(1)}, f32[16,4096]{1,0:T(8,128)}, u32[]{:S(2)}) copy-start(f32[16,4096]{1,0:T(8,128)} %rows_ref.1) | copy-start | bytes 786436
  0.0 37.1 %all-to-all-start = ((bf16[16,8,2,4096]{3,2,1,0:T(2,128)(2,1)}), bf16[16,8,2,4096]{3,2,1,0:T(2,128)(2,1)S(1)}, u32[]{:S(2)}, u32[]{:S(2)}) async-start(bf16[16,8,2,4096]{3,2,1,0:T(2,128)(2,1)} %bitcast.22), calls=%async_computation | async-start | bytes 4194304 | tf_op jit(solution)/shard_map/all_to_all | solution.py:284
  9.8 0.8 copy-start.2
  91.0 15.2 %collective-permute-start.6 = (bf16[2,128,1024]{2,1,0:T(8,128)(2,1)S(1)}, bf16[2,128,1024]{2,1,0:T(8,128)(2,1)S(1)}, u32[]{:S(2)}, u32[]{:S(2)}) collective-permute-start(bf16[2,128,1024]{2,1,0:T(8,128)(2,1)S(1)} %correlate.15), channel_id=1, source_target_pairs={{0,6},{1,7},{2,4},{3,5},{4,2},{5,3},{6,0},{7,1},{8,14},{9,15},{10,... | collective-permute-start | bytes 1572872 | tf_op jit(solution)/shard_map/ppermute | solution.py:296
  92.0 22.6 %collective-permute-start.5 = (bf16[2,128,1024]{2,1,0:T(8,128)(2,1)S(1)}, bf16[2,128,1024]{2,1,0:T(8,128)(2,1)S(1)}, u32[]{:S(2)}, u32[]{:S(2)}) collective-permute-start(bf16[2,128,1024]{2,1,0:T(8,128)(2,1)S(1)} %correlate.13), channel_id=1, source_target_pairs={{0,4},{1,5},{2,6},{3,7},{4,0},{5,1},{6,2},{7,3},{8,12},{9,13},{10,... | collective-permute-start | bytes 1572872 | tf_op jit(solution)/shard_map/ppermute | solution.py:296
  94.1 27.3 %collective-permute-start.4 = (bf16[2,128,1024]{2,1,0:T(8,128)(2,1)S(1)}, bf16[2,128,1024]{2,1,0:T(8,128)(2,1)S(1)}, u32[]{:S(2)}, u32[]{:S(2)}) collective-permute-start(bf16[2,128,1024]{2,1,0:T(8,128)(2,1)S(1)} %correlate.12), channel_id=1, source_target_pairs={{0,2},{1,3},{2,0},{3,1},{4,6},{5,7},{6,4},{7,5},{8,10},{9,11},{10,... | collective-permute-start | bytes 1572872 | tf_op jit(solution)/shard_map/ppermute | solution.py:296
  97.8 41.2 %collective-permute-start.3 = (bf16[2,128,1024]{2,1,0:T(8,128)(2,1)S(1)}, bf16[2,128,1024]{2,1,0:T(8,128)(2,1)S(1)}, u32[]{:S(2)}, u32[]{:S(2)}) collective-permute-start(bf16[2,128,1024]{2,1,0:T(8,128)(2,1)S(1)} %correlate.11), channel_id=1, source_target_pairs={{0,1},{1,0},{2,3},{3,2},{4,5},{5,4},{6,7},{7,6},{8,9},{9,8},{10,11... | collective-permute-start | bytes 1572872 | tf_op jit(solution)/shard_map/ppermute | solution.py:296
  98.9 41.1 %collective-permute-start.2 = (bf16[2,128,1024]{2,1,0:T(8,128)(2,1)S(1)}, bf16[2,128,1024]{2,1,0:T(8,128)(2,1)S(1)}, u32[]{:S(2)}, u32[]{:S(2)}) collective-permute-start(bf16[2,128,1024]{2,1,0:T(8,128)(2,1)S(1)} %correlate.10), channel_id=1, source_target_pairs={{0,5},{1,4},{2,7},{3,6},{4,1},{5,0},{6,3},{7,2},{8,13},{9,12},{10,... | collective-permute-start | bytes 1572872 | tf_op jit(solution)/shard_map/ppermute | solution.py:296
  106.2 33.9 %collective-permute-start.1 = (bf16[2,128,1024]{2,1,0:T(8,128)(2,1)S(1)}, bf16[2,128,1024]{2,1,0:T(8,128)(2,1)S(1)}, u32[]{:S(2)}, u32[]{:S(2)}) collective-permute-start(bf16[2,128,1024]{2,1,0:T(8,128)(2,1)S(1)} %correlate.9), channel_id=1, source_target_pairs={{0,7},{1,6},{2,5},{3,4},{4,3},{5,2},{6,1},{7,0},{8,15},{9,14},{10,... | collective-permute-start | bytes 1572872 | tf_op jit(solution)/shard_map/ppermute | solution.py:296
  114.5 25.6 %collective-permute-start = (bf16[2,128,1024]{2,1,0:T(8,128)(2,1)S(1)}, bf16[2,128,1024]{2,1,0:T(8,128)(2,1)S(1)}, u32[]{:S(2)}, u32[]{:S(2)}) collective-permute-start(bf16[2,128,1024]{2,1,0:T(8,128)(2,1)S(1)} %correlate.8), channel_id=1, source_target_pairs={{0,3},{1,2},{2,1},{3,0},{4,7},{5,6},{6,5},{7,4},{8,11},{9,10},{10,... | collective-permute-start | bytes 1572872 | tf_op jit(solution)/shard_map/ppermute | solution.py:296
